TPU v7x, 32 devices: a whole 2x2x4 slice. The times are simulated.
32 devices in a mesh: groups: 2 (over y), row: 4 (over z), col: 4 (over x, core).
Axes of the slice: x: 2, y: 2, z: 4, core: 2. Of those that a mesh axis runs over, the one named last changes fastest.
Arguments:
- up_a: bfloat16 [4, 4096, 14336], P('groups', 'col', 'row'), parts along dimension 0, may hold values from -2 to 2
- up_b: bfloat16 [4, 4096, 14336], P('groups', ('row', 'col')), parts along dimension 0, may hold values from -2 to 2
- residual_perm: int32 [28672], P('groups'), parts along dimension 0, may hold values from 0 to 14335, each once
- pair_index: int32 [2], P('groups'), parts along dimension 0, may hold values from 0 to 1
Outputs:
- cost: float32 [28672, 14336], P(('groups', 'row'), 'col'), parts along dimension 0
There are 2 independent parts, one for each index of `groups`. A program takes and returns all parts, laid end to end along the dimension named above; each array names one. Nothing has to cross between parts.
Inputs may be any that keep to these rules, and one draw needn't show every extreme that they name: `residual_perm`: each unit of model B appears exactly once.
All inputs are finite; a program needn't handle non-finite values.
Results may differ from a plain program's by a relative error of at most 0.0003.
Values may be sent and summed in bfloat16 or wider, within the bound.
No kernel may reach another device: no remote copies, remote signals or barrier semaphores. Data moves between devices by JAX's collectives and lax.ppermute only.
A program may use at most 320 MiB of HBM per device.

v0:
```python
import jax
import jax.numpy as jnp
from jax import lax
from jax.sharding import PartitionSpec as P


def contract(left, right):
    return lax.dot_general(
        left, right, (((0,), (0,)), ((), ())), preferred_element_type=jnp.float32
    )


def shards(up_a, up_b, residual_perm, pair_index):
    layer = pair_index[0]
    left_units = lax.dynamic_index_in_dim(up_a, layer, 0, keepdims=False)
    right_units = lax.dynamic_index_in_dim(up_b, layer, 0, keepdims=False)
    permuted = jnp.take(right_units, residual_perm, axis=1)
    placed = lax.all_to_all(permuted, "col", split_axis=1, concat_axis=0, tiled=True)
    full_left = lax.all_gather(left_units, "col", axis=0, tiled=True)
    return contract(full_left, lax.all_gather(placed, "row", axis=0, tiled=True))


def solution(mesh):
    placed = (
        P("groups", "col", "row"),
        P("groups", ("row", "col"), None),
        P("groups"),
        P("groups"),
    )
    return jax.shard_map(
        shards, mesh=mesh, in_specs=placed, out_specs=P(("groups", "row"), "col"), check_vma=False
    )
```

profile of v0, /device:TPU:0, one launch (start us, length us, event | category | flops | bytes accessed | tf_op | source)
XLA Modules:
  0.0 893.1 jit_solution(4263160534064428262)
XLA Ops:
  6.5 0.0 all-gather.6.cloned.1.call-start
  7.2 6.5 constant_dynamic-slice_fusion.1
  13.7 0.0 copy-start
  13.7 0.0 all-gather.6.cloned.1.call-update
  13.7 0.0 all-gather.4.cloned.1.call-start
  13.8 0.7 copy-done
  14.6 6.9 constant_dynamic-slice_fusion
  21.5 11.2 %copy.6 = bf16[1,256,14336]{1,2,0:T(8,128)(2,1)} copy(bf16[1,256,14336]{2,1,0:T(8,128)(2,1)} %constant_dynamic-slice_fusion) | data formatting | bytes 14680064 | tf_op jit(solution)/shard_map/jit(dynamic_index_in_dim)/dynamic_slice | solution.py:16
  32.7 59.7 %gather_fusion = bf16[14336,256]{1,0:T(8,128)(2,1)} fusion(bf16[256,14336]{0,1:T(8,128)(2,1)} %bitcast.15, s32[14336]{0:T(1024)S(1)} %fusion.2), kind=kCustom, calls=%fused_computation | custom fusion | bytes 14737408 | tf_op jit(solution)/shard_map/jit(_take)/gather | solution.py:17
  92.5 10.1 %copy.7 = bf16[256,4,3584]{2,0,1:T(8,128)(2,1)} copy(bf16[256,4,3584]{0,2,1:T(8,128)(2,1)} %bitcast.16) | data formatting | bytes 14680064 | tf_op jit(solution)/shard_map/jit(_take)/gather | solution.py:17
  102.5 3.8 broadcast_select_fusion
  106.3 164.3 %all_to_all.16 = bf16[256,4,3584]{2,0,1:T(8,128)(2,1)} all-to-all(bf16[256,4,3584]{2,0,1:T(8,128)(2,1)S(1)} %broadcast_select_fusion), channel_id=1, replica_groups=mesh['groups'=2,'row'=4,'col'=4] {'col'}, dimensions={1} | all-to-all | bytes 14680064 | tf_op jit(solution)/shard_map/all_to_all | solution.py:18
  270.6 0.0 all-gather.4.cloned.1.call-update
  270.7 1.8 all-gather.6.cloned.1.call-done
  272.5 493.9 %all-gather.4.cloned.1.call-done = bf16[4096,3584]{1,0:T(8,128)(2,1)} async-done(((bf16[1024,3584]{1,0:T(8,128)(2,1)}), bf16[4096,3584]{1,0:T(8,128)(2,1)}) %all-gather.4.cloned.1.call-update) | async-done | bytes 29360144 | tf_op jit(solution)/shard_map/all_gather | solution.py:20
  766.4 119.9 %fusion = f32[3584,3584]{1,0:T(8,128)} fusion(bf16[4096,3584]{1,0:T(8,128)(2,1)} %all-gather.4.cloned.1.call-done, bf16[1,4096,3584]{2,1,0:T(8,128)(2,1)} %all-gather.6.cloned.1.call-done), kind=kOutput, calls=%fused_computation.1 | convolution fusion | flops 105226698752 | bytes 110100480 | tf_op jit(solution)/shard_map/dot_general | solution.py:8
  (3 shorter events, 0.1 us)
Async XLA Ops:
  6.5 266.0 %all-gather.6.cloned.1.call-start = ((), (), s32[]{:S(2)}) async-start(), calls=%async_computation.2 | async-start | bytes 36700160 | tf_op jit(solution)/shard_map/all_gather | solution.py:19
  13.7 0.8 copy-start
  13.7 752.6 %all-gather.4.cloned.1.call-start = ((), (), s32[]{:S(2)}) async-start(), calls=%async_computation.1 | async-start | bytes 36700160 | tf_op jit(solution)/shard_map/all_gather | solution.py:20
Sparse Core Ops, SparseCore 0:
  13.9 258.5 all-gather.5
  274.1 492.2 all-gather.3
where the time goes:
time: 894 us; the launch traced here: 893 us
  waiting for transfers between devices  496 us (55%)
  blocking collectives  164 us (18%)
  matrix products  120 us (13%)
  local copies, waits for them, and re-layouts  95.2 us (11%)
  between operations  14.1 us (2%)
    all_gather x1, waiting for transfers between devices, shards(): lax.all_gather(placed, 'row', axis=0, tiled=True)  494 us
    all_to_all x1, blocking collectives, shards(): lax.all_to_all(permuted, 'col', split_axis=1, concat_axis=0, tiled=True)  164 us
    dot_general x1, matrix products, contract(): lax.dot_general(left, right, (((0,), (0,)), ((), ())), preferred_element_...  120 us
    gather x2, local copies, waits for them, and re-layouts, shards(): permuted = jnp.take(right_units, residual_perm, axis=1)  69.8 us
    dynamic_slice x2, local copies, waits for them, and re-layouts, shards(): right_units = lax.dynamic_index_in_dim(up_b, layer, 0, keepdims=False)  18.1 us
  transfers between devices with their start and end apart: 2, of which 2 were waited for; matrix products, arithmetic and copies ran while one was open for 10% of the time, Pallas kernels for 0%

commit v1 on v0

v1 whole, which is shorter than its diff:
```python
import functools

import jax
import jax.numpy as jnp
from jax import lax
from jax.experimental import pallas as pl
from jax.experimental.pallas import tpu as pltpu
from jax.sharding import PartitionSpec as P

LANES = 128
VMEM_LIMIT = 52 * 2**20
WIDTHS = (2, 2, 4, 4, 4, 4, 4, 2, 2)


def widths_of(positions):
    units = positions // LANES
    parts = WIDTHS if sum(WIDTHS) == units else (1,) * units
    return [part * LANES for part in parts]


def select_kernel(slots, layer_ref, units_ref, perm_ref, *refs):
    outs, hot = refs[:slots], refs[slots]
    units = units_ref.shape[2]
    width = outs[0].shape[1]
    step = 1024 if units % 1024 == 0 else units
    for slot in range(slots):
        for start in range(0, width, 256):
            size = min(256, width - start)
            wanted = perm_ref[slot : slot + 1, start : start + size]
            for at in range(0, units, step):
                index = lax.broadcasted_iota(jnp.int32, (step, size), 0) + at
                hot[at : at + step, :size] = jnp.where(index == wanted, 1.0, 0.0).astype(jnp.bfloat16)
            outs[slot][:, start : start + size] = jnp.dot(
                units_ref[0], hot[:, :size], preferred_element_type=jnp.float32
            ).astype(jnp.bfloat16)


def select_units(up_b, layer, perms, width):
    slots = perms.shape[0]
    _, features, units = up_b.shape
    return pl.pallas_call(
        functools.partial(select_kernel, slots),
        out_shape=[jax.ShapeDtypeStruct((features, width), jnp.bfloat16)] * slots,
        grid_spec=pltpu.PrefetchScalarGridSpec(
            num_scalar_prefetch=1,
            grid=(1,),
            in_specs=[
                pl.BlockSpec((1, features, units), lambda i, layer: (layer[0], 0, 0)),
                pl.BlockSpec((slots, width), lambda i, layer: (0, 0)),
            ],
            out_specs=[pl.BlockSpec((features, width), lambda i, layer: (0, 0))] * slots,
            scratch_shapes=[pltpu.VMEM((units, 256), jnp.bfloat16)],
        ),
        compiler_params=pltpu.CompilerParams(vmem_limit_bytes=VMEM_LIMIT),
        cost_estimate=pl.CostEstimate(
            flops=2 * features * units * width * slots,
            bytes_accessed=2 * features * (units + width * slots),
            transcendentals=0,
        ),
        name="select_units",
    )(layer, up_b, perms)


def place_kernel(slots, at_ref, *refs):
    out = refs[slots]
    for slot in range(slots):
        out[at_ref[slot]] = refs[slot][...]


def place(at, blocks):
    slots = len(blocks)
    features, width = blocks[0].shape
    whole = pl.BlockSpec((features, width), lambda i, at: (0, 0))
    return pl.pallas_call(
        functools.partial(place_kernel, slots),
        out_shape=jax.ShapeDtypeStruct((slots, features, width), jnp.bfloat16),
        grid_spec=pltpu.PrefetchScalarGridSpec(
            num_scalar_prefetch=1,
            grid=(1,),
            in_specs=[whole] * slots,
            out_specs=pl.BlockSpec((slots, features, width), lambda i, at: (0, 0, 0)),
        ),
        compiler_params=pltpu.CompilerParams(vmem_limit_bytes=VMEM_LIMIT),
        cost_estimate=pl.CostEstimate(
            flops=0, bytes_accessed=4 * slots * features * width, transcendentals=0
        ),
        name="place",
    )(at, *blocks).reshape(slots * features, width)


def turn_kernel(layer_ref, units_ref, after_ref, out_ref):
    out_ref[...] = units_ref[0].T


def turn(up_a, layer, after):
    _, features, units = up_a.shape
    tile = 512 if units % 512 == 0 else 256
    return pl.pallas_call(
        turn_kernel,
        out_shape=jax.ShapeDtypeStruct((units, features), jnp.bfloat16),
        grid_spec=pltpu.PrefetchScalarGridSpec(
            num_scalar_prefetch=1,
            grid=(units // tile,),
            in_specs=[
                pl.BlockSpec((1, features, tile), lambda i, layer: (layer[0], 0, i)),
                pl.BlockSpec(memory_space=pl.ANY),
            ],
            out_specs=pl.BlockSpec((tile, features), lambda i, layer: (i, 0)),
        ),
        compiler_params=pltpu.CompilerParams(vmem_limit_bytes=VMEM_LIMIT),
        cost_estimate=pl.CostEstimate(
            flops=0, bytes_accessed=4 * features * units, transcendentals=0
        ),
        name="turn",
    )(layer, up_a, after)


def product_kernel(pieces, blocks, places, at_ref, *refs):
    lefts, rights, out = refs[:pieces], refs[pieces : pieces + blocks], refs[-1]
    depth = lefts[0].shape[2]
    total = None
    for piece, (block, row) in enumerate(places):
        term = jnp.dot(
            lefts[piece][0],
            rights[block][row : row + depth, :],
            preferred_element_type=jnp.float32,
        )
        total = term if total is None else total + term
    out[...] = total


def product(left, at, rights, cost, offset, positions):
    shares, units, share = left.shape
    blocks = len(rights)
    block, width = rights[0].shape
    depth = min(share, block)
    per_block = block // depth
    tile = 512 if units % 512 == 0 else 256
    column = offset // width
    places = [(k, t * depth) for k in range(blocks) for t in range(per_block)]

    def left_at(k, row, i, at):
        feature = at[k] * block + row
        return (feature // share, i, (feature % share) // depth)

    in_specs = [
        pl.BlockSpec((1, tile, depth), functools.partial(left_at, k, row)) for k, row in places
    ] + [pl.BlockSpec((block, width), lambda i, at: (0, 0))] * blocks
    operands = [left] * len(places) + list(rights)
    aliases = {}
    if cost is not None:
        in_specs.append(pl.BlockSpec(memory_space=pl.ANY))
        operands.append(cost)
        aliases = {len(operands): 0}
    return pl.pallas_call(
        functools.partial(product_kernel, len(places), blocks, places),
        out_shape=jax.ShapeDtypeStruct((units, positions), jnp.float32),
        grid_spec=pltpu.PrefetchScalarGridSpec(
            num_scalar_prefetch=1,
            grid=(units // tile,),
            in_specs=in_specs,
            out_specs=pl.BlockSpec((tile, width), lambda i, at: (i, column)),
        ),
        input_output_aliases=aliases,
        compiler_params=pltpu.CompilerParams(vmem_limit_bytes=VMEM_LIMIT),
        cost_estimate=pl.CostEstimate(
            flops=2 * units * width * block * blocks,
            bytes_accessed=2 * shares * share * units + 2 * block * blocks * width + 4 * units * width,
            transcendentals=0,
        ),
        name="product",
    )(at, *operands)


def exchange(sent, cols):
    back = [sent[0]]
    for s in range(1, cols):
        if cols & (cols - 1) == 0:
            pairs = [(i, i ^ s) for i in range(cols)]
        else:
            pairs = [(i, (i + s) % cols) for i in range(cols)]
        back.append(lax.ppermute(sent[s], "col", pairs))
    return back


def gather_rows(own, rows):
    if rows != 4:
        shifted = [
            lax.ppermute(own, "row", [(i, (i + s) % rows) for i in range(rows)])
            for s in range(1, rows)
        ]
        return [own] + shifted
    ahead = lax.ppermute(own, "row", [(0, 1), (1, 2), (2, 3), (3, 0)])
    behind = lax.ppermute(own, "row", [(1, 0), (2, 1), (3, 2), (0, 3)])
    onward = lax.select(lax.axis_index("row") % 2 == 1, behind, ahead)
    across = lax.ppermute(onward, "row", [(0, 1), (1, 0), (2, 3), (3, 2)])
    return [own, ahead, across, behind]


def solution(mesh):
    rows, cols = mesh.shape["row"], mesh.shape["col"]

    def shards(up_a, up_b, residual_perm, pair_index):
        r, c = lax.axis_index("row"), lax.axis_index("col")
        layer = pair_index
        positions = residual_perm.shape[0] // cols
        steps = jnp.arange(cols, dtype=jnp.int32)
        if cols & (cols - 1) == 0:
            to, come = c ^ steps, c ^ steps
        else:
            to, come = (c + steps) % cols, (c - steps) % cols
        perms = jnp.take(residual_perm.reshape(cols, positions), to, axis=0)
        at = (r - jnp.arange(rows, dtype=jnp.int32)) % rows

        left, cost, offset = None, None, 0
        for width in widths_of(positions):
            wanted = lax.slice_in_dim(perms, offset, offset + width, axis=1)
            back = exchange(select_units(up_b, layer, wanted, width), cols)
            own = place(come, back)
            if left is None:
                left = lax.all_gather(turn(up_a, layer, own), "col", axis=0)
            cost = product(left, at, gather_rows(own, rows), cost, offset, positions)
            offset += width
        return cost

    placed = (
        P("groups", "col", "row"),
        P("groups", ("row", "col"), None),
        P("groups"),
        P("groups"),
    )
    return jax.shard_map(
        shards, mesh=mesh, in_specs=placed, out_specs=P(("groups", "row"), "col"), check_vma=False
    )
```

time: 894 us -> 746 us (0.83)
  Pallas kernels: 0 us -> 333 us
  waiting for transfers between devices: 496 us -> 207 us
  blocking collectives: 164 us -> 0 us
  starting transfers between devices: 0.04 us -> 156 us
  matrix products: 120 us -> 0 us
  local copies, waits for them, and re-layouts: 95.2 us -> 17.6 us
    all_gather x2 -> x1, waiting for transfers between devices: 496 us -> 0.01 us  [shards(): left = lax.all_gather(turn(up_a, layer, own), 'col', axis=0)]
    pallas_call x0 -> x28, Pallas kernels: none -> 333 us  [the longest x9 174 us: product(): pl.pallas_call(functools.partial(product_kernel, len(places), blocks, pla...]
    ppermute x0 -> x54, waiting for transfers between devices: none -> 207 us  [the longest x9 98.6 us: gather_rows(): ahead = lax.ppermute(own, 'row', [(0, 1), (1, 2), (2, 3), (3, 0)])]
    all_to_all x1 -> x0, blocking collectives: 164 us -> none  [shards(): lax.all_to_all(permuted, 'col', split_axis=1, concat_axis=0, tiled=True)]
    ppermute x0 -> x54, starting transfers between devices: none -> 156 us  [the longest x9 104 us: gather_rows(): behind = lax.ppermute(own, 'row', [(1, 0), (2, 1), (3, 2), (0, 3)])]
    dot_general x1 -> x0, matrix products: 120 us -> none  [contract(): lax.dot_general(left, right, (((0,), (0,)), ((), ())), preferred_element_...]
    gather x2 -> x1, local copies, waits for them, and re-layouts: 69.8 us -> 0.58 us  [shards(): perms = jnp.take(residual_perm.reshape(cols, positions), to, axis=0)]
    dynamic_slice x3 -> x0, local copies, waits for them, and re-layouts: 24.6 us -> none  [the longest x2 18.1 us: shards(): right_units = lax.dynamic_index_in_dim(up_b, layer, 0, keepdims=False)]
  transfers between devices with their start and end apart: 2 -> 55, of which waited for: 2 -> 22; matrix products, arithmetic and copies ran while one was open for 10% -> 2% of each run, Pallas kernels for 0% -> 40%
where the time goes in v1:
time: 746 us; the launch traced here: 740 us
  Pallas kernels  333 us (45%)
  waiting for transfers between devices  207 us (28%)
  starting transfers between devices  156 us (21%)
  local copies, waits for them, and re-layouts  17.6 us (2%)
  between operations  14.7 us (2%)
  other arithmetic  12 us (2%)
    pallas_call x9, Pallas kernels, product(): pl.pallas_call(functools.partial(product_kernel, len(places), blocks, pla...  174 us
    pallas_call x9, Pallas kernels, select_units(): pl.pallas_call(functools.partial(select_kernel, slots), out_shape=[jax.Sh...  139 us
    ppermute x9, starting transfers between devices, gather_rows(): behind = lax.ppermute(own, 'row', [(1, 0), (2, 1), (3, 2), (0, 3)])  104 us
    ppermute x9, waiting for transfers between devices, gather_rows(): ahead = lax.ppermute(own, 'row', [(0, 1), (1, 2), (2, 3), (3, 0)])  98.6 us
    ppermute x27, waiting for transfers between devices, exchange(): back.append(lax.ppermute(sent[s], 'col', pairs))  55 us
    ppermute x9, waiting for transfers between devices, gather_rows(): across = lax.ppermute(onward, 'row', [(0, 1), (1, 0), (2, 3), (3, 2)])  29.7 us
    ppermute x9, starting transfers between devices, gather_rows(): across = lax.ppermute(onward, 'row', [(0, 1), (1, 0), (2, 3), (3, 2)])  25.7 us
    ppermute x9, waiting for transfers between devices, gather_rows(): behind = lax.ppermute(own, 'row', [(1, 0), (2, 1), (3, 2), (0, 3)])  23.3 us
  transfers between devices with their start and end apart: 55, of which 22 were waited for; matrix products, arithmetic and copies ran while one was open for 2% of the time, Pallas kernels for 40%

profile of v1, /device:TPU:0, one launch (start us, length us, event | category | flops | bytes accessed | tf_op | source)
XLA Modules:
  0.0 739.8 jit_solution(8691200300947459285)
XLA Ops:
  66.9 19.1 %select_units.16 = (bf16[256,512]{1,0:T(8,128)(2,1)S(1)}, bf16[256,512]{1,0:T(8,128)(2,1)S(1)}, bf16[256,512]{1,0:T(8,128)(2,1)S(1)}, bf16[256,512]{1,0:T(8,128)(2,1)S(1)}) custom-call(s32[1]{0:T(128)S(6)} %copy.21.layer_ref, bf16[2,256,14336]{2,1,0:T(8,128)(2,1)} %units_ref.19, s32[4,512]{1,0:T(4,128)S(1)} %get-tuple-element.81.perm_ref), custom_call_target="tpu_custom_call" | custom-call | flops 15032385536 | bytes 8388608 | tf_op jit(solution)/shard_map/select_units/pallas_call | solution.py:41
  85.9 18.7 %select_units.15 = (bf16[256,512]{1,0:T(8,128)(2,1)S(1)}, bf16[256,512]{1,0:T(8,128)(2,1)S(1)}, bf16[256,512]{1,0:T(8,128)(2,1)S(1)}, bf16[256,512]{1,0:T(8,128)(2,1)S(1)}) custom-call(s32[1]{0:T(128)S(6)} %copy.21.layer_ref, bf16[2,256,14336]{2,1,0:T(8,128)(2,1)} %units_ref.19, s32[4,512]{1,0:T(4,128)S(1)} %get-tuple-element.82.perm_ref), custom_call_target="tpu_custom_call" | custom-call | flops 15032385536 | bytes 8388608 | tf_op jit(solution)/shard_map/select_units/pallas_call | solution.py:41
  119.8 18.7 %select_units.14 = (bf16[256,512]{1,0:T(8,128)(2,1)S(1)}, bf16[256,512]{1,0:T(8,128)(2,1)S(1)}, bf16[256,512]{1,0:T(8,128)(2,1)S(1)}, bf16[256,512]{1,0:T(8,128)(2,1)S(1)}) custom-call(s32[1]{0:T(128)S(6)} %copy.21.layer_ref, bf16[2,256,14336]{2,1,0:T(8,128)(2,1)} %units_ref.19, s32[4,512]{1,0:T(4,128)S(1)} %get-tuple-element.83.perm_ref), custom_call_target="tpu_custom_call" | custom-call | flops 15032385536 | bytes 8388608 | tf_op jit(solution)/shard_map/select_units/pallas_call | solution.py:41
  144.0 18.9 %select_units.13 = (bf16[256,512]{1,0:T(8,128)(2,1)S(1)}, bf16[256,512]{1,0:T(8,128)(2,1)S(1)}, bf16[256,512]{1,0:T(8,128)(2,1)S(1)}, bf16[256,512]{1,0:T(8,128)(2,1)S(1)}) custom-call(s32[1]{0:T(128)S(6)} %copy.21.layer_ref, bf16[2,256,14336]{2,1,0:T(8,128)(2,1)} %units_ref.19, s32[4,512]{1,0:T(4,128)S(1)} %get-tuple-element.84.perm_ref), custom_call_target="tpu_custom_call" | custom-call | flops 15032385536 | bytes 8388608 | tf_op jit(solution)/shard_map/select_units/pallas_call | solution.py:41
  177.6 18.6 %select_units.12 = (bf16[256,512]{1,0:T(8,128)(2,1)S(1)}, bf16[256,512]{1,0:T(8,128)(2,1)S(1)}, bf16[256,512]{1,0:T(8,128)(2,1)S(1)}, bf16[256,512]{1,0:T(8,128)(2,1)S(1)}) custom-call(s32[1]{0:T(128)S(6)} %copy.21.layer_ref, bf16[2,256,14336]{2,1,0:T(8,128)(2,1)} %units_ref.19, s32[4,512]{1,0:T(4,128)S(1)} %get-tuple-element.85.perm_ref), custom_call_target="tpu_custom_call" | custom-call | flops 15032385536 | bytes 8388608 | tf_op jit(solution)/shard_map/select_units/pallas_call | solution.py:41
  301.1 18.8 %collective-permute-done.42.refs_5_ = bf16[1024,512]{1,0:T(8,128)(2,1)} collective-permute-done((bf16[1024,512]{1,0:T(8,128)(2,1)}, bf16[1024,512]{1,0:T(8,128)(2,1)}, u32[]{:S(2)}, u32[]{:S(2)}) %collective-permute-start.42) | collective-permute-done | bytes 1048608 | tf_op jit(solution)/shard_map/ppermute | solution.py:193
  319.8 24.3 %collective-permute-start.31 = (bf16[1024,512]{1,0:T(8,128)(2,1)}, bf16[1024,512]{1,0:T(8,128)(2,1)S(1)}, u32[]{:S(2)}, u32[]{:S(2)}) collective-permute-start(bf16[1024,512]{1,0:T(8,128)(2,1)} %bitcast.29), channel_id=1, source_target_pairs={{4,0},{8,4},{12,8},{0,12},{5,1},{9,5},{13,9},{1,13},{6,2},{10,6},{... | collective-permute-start | bytes 3145736 | tf_op jit(solution)/shard_map/ppermute | solution.py:194
  345.0 19.8 %collective-permute-done.36.refs_5_ = bf16[1024,512]{1,0:T(8,128)(2,1)} collective-permute-done((bf16[1024,512]{1,0:T(8,128)(2,1)}, bf16[1024,512]{1,0:T(8,128)(2,1)}, u32[]{:S(2)}, u32[]{:S(2)}) %collective-permute-start.36) | collective-permute-done | bytes 1048608 | tf_op jit(solution)/shard_map/ppermute | solution.py:193
  364.8 24.2 %collective-permute-start.25 = (bf16[1024,512]{1,0:T(8,128)(2,1)}, bf16[1024,512]{1,0:T(8,128)(2,1)S(1)}, u32[]{:S(2)}, u32[]{:S(2)}) collective-permute-start(bf16[1024,512]{1,0:T(8,128)(2,1)} %bitcast.26), channel_id=1, source_target_pairs={{4,0},{8,4},{12,8},{0,12},{5,1},{9,5},{13,9},{1,13},{6,2},{10,6},{... | collective-permute-start | bytes 3145736 | tf_op jit(solution)/shard_map/ppermute | solution.py:194
  390.0 19.7 %collective-permute-done.30.refs_5_ = bf16[1024,512]{1,0:T(8,128)(2,1)S(1)} collective-permute-done((bf16[1024,512]{1,0:T(8,128)(2,1)}, bf16[1024,512]{1,0:T(8,128)(2,1)S(1)}, u32[]{:S(2)}, u32[]{:S(2)}) %collective-permute-start.30) | collective-permute-done | bytes 1048608 | tf_op jit(solution)/shard_map/ppermute | solution.py:193
  409.7 24.3 %collective-permute-start.19 = (bf16[1024,512]{1,0:T(8,128)(2,1)}, bf16[1024,512]{1,0:T(8,128)(2,1)S(1)}, u32[]{:S(2)}, u32[]{:S(2)}) collective-permute-start(bf16[1024,512]{1,0:T(8,128)(2,1)} %bitcast.23), channel_id=1, source_target_pairs={{4,0},{8,4},{12,8},{0,12},{5,1},{9,5},{13,9},{1,13},{6,2},{10,6},{... | collective-permute-start | bytes 3145736 | tf_op jit(solution)/shard_map/ppermute | solution.py:194
  454.7 20.6 %collective-permute-start.50 = (bf16[1024,256]{1,0:T(8,128)(2,1)}, bf16[1024,256]{1,0:T(8,128)(2,1)}, u32[]{:S(2)}, u32[]{:S(2)}) collective-permute-start(bf16[1024,256]{1,0:T(8,128)(2,1)} %broadcast_select_fusion.6), channel_id=1, source_target_pairs={{0,4},{4,0},{8,12},{12,8},{1,5},{5,1},{9,13},{13,9},{2,6},{6,2},{1... | collective-permute-start | bytes 1572872 | tf_op jit(solution)/shard_map/ppermute | solution.py:196
  478.5 21.2 %collective-permute-done.18.refs_5_ = bf16[1024,512]{1,0:T(8,128)(2,1)S(1)} collective-permute-done((bf16[1024,512]{1,0:T(8,128)(2,1)}, bf16[1024,512]{1,0:T(8,128)(2,1)S(1)}, u32[]{:S(2)}, u32[]{:S(2)}) %collective-permute-start.18) | collective-permute-done | bytes 1048608 | tf_op jit(solution)/shard_map/ppermute | solution.py:193
  499.7 21.7 %collective-permute-done.19.refs_7_ = bf16[1024,512]{1,0:T(8,128)(2,1)S(1)} collective-permute-done((bf16[1024,512]{1,0:T(8,128)(2,1)}, bf16[1024,512]{1,0:T(8,128)(2,1)S(1)}, u32[]{:S(2)}, u32[]{:S(2)}) %collective-permute-start.19) | collective-permute-done | bytes 1048608 | tf_op jit(solution)/shard_map/ppermute | solution.py:194
  535.2 16.2 %product.9.refs_8_ = f32[3584,3584]{1,0:T(8,128)} custom-call(s32[4]{0:T(128)S(1)} %and_select_fusion.at_ref, bf16[4,3584,1024]{2,1,0:T(8,128)(2,1)} %bitcast.40, bf16[4,3584,1024]{2,1,0:T(8,128)(2,1)} %bitcast.41, bf16[4,3584,1024]{2,1,0:T(8,128)(2,1)} %bitcast.42, bf16[4,3584,1024]{2,1,0:T(8,128)(2,1)} %bitcast.43, bf16[1024,256]{1,0:T(8,128)(2,1)S(1)} %bitcast.15, ...), custom_call_target="tpu_custom_call" | custom-call | flops 7516192768 | bytes 35127296 | tf_op jit(solution)/shard_map/product/pallas_call | solution.py:155
  552.9 16.4 %product.10.refs_8_ = f32[3584,3584]{1,0:T(8,128)} custom-call(s32[4]{0:T(128)S(1)} %and_select_fusion.at_ref, bf16[4,3584,1024]{2,1,0:T(8,128)(2,1)} %bitcast.44, bf16[4,3584,1024]{2,1,0:T(8,128)(2,1)} %bitcast.45, bf16[4,3584,1024]{2,1,0:T(8,128)(2,1)} %bitcast.46, bf16[4,3584,1024]{2,1,0:T(8,128)(2,1)} %bitcast.47, ...), custom_call_target="tpu_custom_call", output_to_operand_aliasing={{}: (9, {})} | custom-call | flops 7516192768 | bytes 35127296 | tf_op jit(solution)/shard_map/product/pallas_call | solution.py:155
  569.3 19.7 %collective-permute-done.44.refs_6_ = bf16[1024,512]{1,0:T(8,128)(2,1)} collective-permute-done((bf16[1024,512]{1,0:T(8,128)(2,1)}, bf16[1024,512]{1,0:T(8,128)(2,1)}, u32[]{:S(2)}, u32[]{:S(2)}) %collective-permute-start.44) | collective-permute-done | bytes 1048608 | tf_op jit(solution)/shard_map/ppermute | solution.py:196
  589.6 21.7 %product.11.refs_8_ = f32[3584,3584]{1,0:T(8,128)} custom-call(s32[4]{0:T(128)S(1)} %and_select_fusion.at_ref, bf16[4,3584,1024]{2,1,0:T(8,128)(2,1)} %bitcast.48, bf16[4,3584,1024]{2,1,0:T(8,128)(2,1)} %bitcast.49, bf16[4,3584,1024]{2,1,0:T(8,128)(2,1)} %bitcast.50, bf16[4,3584,1024]{2,1,0:T(8,128)(2,1)} %bitcast.51, ...), custom_call_target="tpu_custom_call", output_to_operand_aliasing={{}: (9, {})} | custom-call | flops 15032385536 | bytes 40894464 | tf_op jit(solution)/shard_map/product/pallas_call | solution.py:155
  612.8 21.7 %product.12.refs_8_ = f32[3584,3584]{1,0:T(8,128)} custom-call(s32[4]{0:T(128)S(1)} %and_select_fusion.at_ref, bf16[4,3584,1024]{2,1,0:T(8,128)(2,1)} %bitcast.52, bf16[4,3584,1024]{2,1,0:T(8,128)(2,1)} %bitcast.53, bf16[4,3584,1024]{2,1,0:T(8,128)(2,1)} %bitcast.54, bf16[4,3584,1024]{2,1,0:T(8,128)(2,1)} %bitcast.55, ...), custom_call_target="tpu_custom_call", output_to_operand_aliasing={{}: (9, {})} | custom-call | flops 15032385536 | bytes 40894464 | tf_op jit(solution)/shard_map/product/pallas_call | solution.py:155
  634.5 21.7 %product.13.refs_8_ = f32[3584,3584]{1,0:T(8,128)} custom-call(s32[4]{0:T(128)S(1)} %and_select_fusion.at_ref, bf16[4,3584,1024]{2,1,0:T(8,128)(2,1)} %bitcast.57, bf16[4,3584,1024]{2,1,0:T(8,128)(2,1)} %bitcast.56, bf16[4,3584,1024]{2,1,0:T(8,128)(2,1)} %bitcast.58, bf16[4,3584,1024]{2,1,0:T(8,128)(2,1)} %bitcast.59, ...), custom_call_target="tpu_custom_call", output_to_operand_aliasing={{}: (9, {})} | custom-call | flops 15032385536 | bytes 40894464 | tf_op jit(solution)/shard_map/product/pallas_call | solution.py:155
  656.4 21.7 %product.14.refs_8_ = f32[3584,3584]{1,0:T(8,128)} custom-call(s32[4]{0:T(128)S(1)} %and_select_fusion.at_ref, bf16[4,3584,1024]{2,1,0:T(8,128)(2,1)} %bitcast.60, bf16[4,3584,1024]{2,1,0:T(8,128)(2,1)} %bitcast.61, bf16[4,3584,1024]{2,1,0:T(8,128)(2,1)} %bitcast.62, bf16[4,3584,1024]{2,1,0:T(8,128)(2,1)} %bitcast.63, ...), custom_call_target="tpu_custom_call", output_to_operand_aliasing={{}: (9, {})} | custom-call | flops 15032385536 | bytes 40894464 | tf_op jit(solution)/shard_map/product/pallas_call | solution.py:155
  678.2 21.7 %product.15.refs_8_ = f32[3584,3584]{1,0:T(8,128)} custom-call(s32[4]{0:T(128)S(1)} %and_select_fusion.at_ref, bf16[4,3584,1024]{2,1,0:T(8,128)(2,1)} %bitcast.64, bf16[4,3584,1024]{2,1,0:T(8,128)(2,1)} %bitcast.65, bf16[4,3584,1024]{2,1,0:T(8,128)(2,1)} %bitcast.66, bf16[4,3584,1024]{2,1,0:T(8,128)(2,1)} %bitcast.67, ...), custom_call_target="tpu_custom_call", output_to_operand_aliasing={{}: (9, {})} | custom-call | flops 15032385536 | bytes 40894464 | tf_op jit(solution)/shard_map/product/pallas_call | solution.py:155
  699.9 16.4 %product.16.refs_8_ = f32[3584,3584]{1,0:T(8,128)} custom-call(s32[4]{0:T(128)S(1)} %and_select_fusion.at_ref, bf16[4,3584,1024]{2,1,0:T(8,128)(2,1)} %bitcast.68, bf16[4,3584,1024]{2,1,0:T(8,128)(2,1)} %bitcast.69, bf16[4,3584,1024]{2,1,0:T(8,128)(2,1)} %bitcast.70, bf16[4,3584,1024]{2,1,0:T(8,128)(2,1)} %bitcast.71, ...), custom_call_target="tpu_custom_call", output_to_operand_aliasing={{}: (9, {})} | custom-call | flops 7516192768 | bytes 35127296 | tf_op jit(solution)/shard_map/product/pallas_call | solution.py:155
  716.3 16.4 %product.17 = f32[3584,3584]{1,0:T(8,128)} custom-call(s32[4]{0:T(128)S(1)} %and_select_fusion.at_ref, bf16[4,3584,1024]{2,1,0:T(8,128)(2,1)} %bitcast.72, bf16[4,3584,1024]{2,1,0:T(8,128)(2,1)} %bitcast.73, bf16[4,3584,1024]{2,1,0:T(8,128)(2,1)} %bitcast.74, bf16[4,3584,1024]{2,1,0:T(8,128)(2,1)} %bitcast.75, ...), custom_call_target="tpu_custom_call", output_to_operand_aliasing={{}: (9, {})} | custom-call | flops 7516192768 | bytes 35127296 | tf_op jit(solution)/shard_map/product/pallas_call | solution.py:155
  (220 shorter events, 242.8 us)
Async XLA Ops:
  6.5 527.6 %all-gather.3.cloned.1.call-start = ((), (), s32[]{:S(2)}) async-start(), calls=%async_computation | async-start | bytes 36700160 | tf_op jit(solution)/shard_map/all_gather | solution.py:221
  50.5 54.1 %collective-permute-start.45 = (bf16[256,256]{1,0:T(8,128)(2,1)S(1)}, bf16[256,256]{1,0:T(8,128)(2,1)S(1)}, u32[]{:S(2)}, u32[]{:S(2)}) collective-permute-start(bf16[256,256]{1,0:T(8,128)(2,1)S(1)} %get-tuple-element.74), channel_id=1, source_target_pairs={{0,1},{1,0},{2,3},{3,2},{4,5},{5,4},{6,7},{7,6},{8,9},{9,8},{10,11... | collective-permute-start | bytes 393224 | tf_op jit(solution)/shard_map/ppermute | solution.py:182
  50.7 65.4 %collective-permute-start.46 = (bf16[256,256]{1,0:T(8,128)(2,1)S(1)}, bf16[256,256]{1,0:T(8,128)(2,1)S(1)}, u32[]{:S(2)}, u32[]{:S(2)}) collective-permute-start(bf16[256,256]{1,0:T(8,128)(2,1)S(1)} %get-tuple-element.75), channel_id=1, source_target_pairs={{0,2},{1,3},{2,0},{3,1},{4,6},{5,7},{6,4},{7,5},{8,10},{9,11},{10,... | collective-permute-start | bytes 393224 | tf_op jit(solution)/shard_map/ppermute | solution.py:182
  52.4 63.9 %collective-permute-start.47 = (bf16[256,256]{1,0:T(8,128)(2,1)S(1)}, bf16[256,256]{1,0:T(8,128)(2,1)S(1)}, u32[]{:S(2)}, u32[]{:S(2)}) collective-permute-start(bf16[256,256]{1,0:T(8,128)(2,1)S(1)} %get-tuple-element.76), channel_id=1, source_target_pairs={{0,3},{1,2},{2,1},{3,0},{4,7},{5,6},{6,5},{7,4},{8,11},{9,10},{10,... | collective-permute-start | bytes 393224 | tf_op jit(solution)/shard_map/ppermute | solution.py:182
  65.0 52.9 %collective-permute-start.10 = (bf16[256,256]{1,0:T(8,128)(2,1)S(1)}, bf16[256,256]{1,0:T(8,128)(2,1)S(1)}, u32[]{:S(2)}, u32[]{:S(2)}) collective-permute-start(bf16[256,256]{1,0:T(8,128)(2,1)S(1)} %get-tuple-element.51), channel_id=1, source_target_pairs={{0,2},{1,3},{2,0},{3,1},{4,6},{5,7},{6,4},{7,5},{8,10},{9,11},{10,... | collective-permute-start | bytes 393224 | tf_op jit(solution)/shard_map/ppermute | solution.py:182
  257.6 62.2 %collective-permute-start.42 = (bf16[1024,512]{1,0:T(8,128)(2,1)}, bf16[1024,512]{1,0:T(8,128)(2,1)}, u32[]{:S(2)}, u32[]{:S(2)}) collective-permute-start(bf16[1024,512]{1,0:T(8,128)(2,1)} %bitcast.19), channel_id=1, source_target_pairs={{0,4},{4,8},{8,12},{12,0},{1,5},{5,9},{9,13},{13,1},{2,6},{6,10},{... | collective-permute-start | bytes 3145736 | tf_op jit(solution)/shard_map/ppermute | solution.py:193
  263.5 81.5 %collective-permute-start.43 = (bf16[1024,512]{1,0:T(8,128)(2,1)}, bf16[1024,512]{1,0:T(8,128)(2,1)}, u32[]{:S(2)}, u32[]{:S(2)}) collective-permute-start(bf16[1024,512]{1,0:T(8,128)(2,1)} %bitcast.20), channel_id=1, source_target_pairs={{4,0},{8,4},{12,8},{0,12},{5,1},{9,5},{13,9},{1,13},{6,2},{10,6},{... | collective-permute-start | bytes 3145736 | tf_op jit(solution)/shard_map/ppermute | solution.py:194
  277.4 87.5 %collective-permute-start.36 = (bf16[1024,512]{1,0:T(8,128)(2,1)}, bf16[1024,512]{1,0:T(8,128)(2,1)}, u32[]{:S(2)}, u32[]{:S(2)}) collective-permute-start(bf16[1024,512]{1,0:T(8,128)(2,1)} %bitcast.16), channel_id=1, source_target_pairs={{0,4},{4,8},{8,12},{12,0},{1,5},{5,9},{9,13},{13,1},{2,6},{6,10},{... | collective-permute-start | bytes 3145736 | tf_op jit(solution)/shard_map/ppermute | solution.py:193
  292.7 97.3 %collective-permute-start.37 = (bf16[1024,512]{1,0:T(8,128)(2,1)}, bf16[1024,512]{1,0:T(8,128)(2,1)S(1)}, u32[]{:S(2)}, u32[]{:S(2)}) collective-permute-start(bf16[1024,512]{1,0:T(8,128)(2,1)} %bitcast.17), channel_id=1, source_target_pairs={{4,0},{8,4},{12,8},{0,12},{5,1},{9,5},{13,9},{1,13},{6,2},{10,6},{... | collective-permute-start | bytes 3145736 | tf_op jit(solution)/shard_map/ppermute | solution.py:194
  299.1 110.7 %collective-permute-start.30 = (bf16[1024,512]{1,0:T(8,128)(2,1)}, bf16[1024,512]{1,0:T(8,128)(2,1)S(1)}, u32[]{:S(2)}, u32[]{:S(2)}) collective-permute-start(bf16[1024,512]{1,0:T(8,128)(2,1)} %bitcast.28), channel_id=1, source_target_pairs={{0,4},{4,8},{8,12},{12,0},{1,5},{5,9},{9,13},{13,1},{2,6},{6,10},{... | collective-permute-start | bytes 3145736 | tf_op jit(solution)/shard_map/ppermute | solution.py:193
  319.8 118.8 %collective-permute-start.31 = (bf16[1024,512]{1,0:T(8,128)(2,1)}, bf16[1024,512]{1,0:T(8,128)(2,1)S(1)}, u32[]{:S(2)}, u32[]{:S(2)}) collective-permute-start(bf16[1024,512]{1,0:T(8,128)(2,1)} %bitcast.29), channel_id=1, source_target_pairs={{4,0},{8,4},{12,8},{0,12},{5,1},{9,5},{13,9},{1,13},{6,2},{10,6},{... | collective-permute-start | bytes 3145736 | tf_op jit(solution)/shard_map/ppermute | solution.py:194
  345.0 109.7 %collective-permute-start.24 = (bf16[1024,512]{1,0:T(8,128)(2,1)}, bf16[1024,512]{1,0:T(8,128)(2,1)S(1)}, u32[]{:S(2)}, u32[]{:S(2)}) collective-permute-start(bf16[1024,512]{1,0:T(8,128)(2,1)} %bitcast.25), channel_id=1, source_target_pairs={{0,4},{4,8},{8,12},{12,0},{1,5},{5,9},{9,13},{13,1},{2,6},{6,10},{... | collective-permute-start | bytes 3145736 | tf_op jit(solution)/shard_map/ppermute | solution.py:193
  364.8 112.0 %collective-permute-start.25 = (bf16[1024,512]{1,0:T(8,128)(2,1)}, bf16[1024,512]{1,0:T(8,128)(2,1)S(1)}, u32[]{:S(2)}, u32[]{:S(2)}) collective-permute-start(bf16[1024,512]{1,0:T(8,128)(2,1)} %bitcast.26), channel_id=1, source_target_pairs={{4,0},{8,4},{12,8},{0,12},{5,1},{9,5},{13,9},{1,13},{6,2},{10,6},{... | collective-permute-start | bytes 3145736 | tf_op jit(solution)/shard_map/ppermute | solution.py:194
  390.0 109.7 %collective-permute-start.18 = (bf16[1024,512]{1,0:T(8,128)(2,1)}, bf16[1024,512]{1,0:T(8,128)(2,1)S(1)}, u32[]{:S(2)}, u32[]{:S(2)}) collective-permute-start(bf16[1024,512]{1,0:T(8,128)(2,1)} %bitcast.22), channel_id=1, source_target_pairs={{0,4},{4,8},{8,12},{12,0},{1,5},{5,9},{9,13},{13,1},{2,6},{6,10},{... | collective-permute-start | bytes 3145736 | tf_op jit(solution)/shard_map/ppermute | solution.py:193
  409.7 111.7 %collective-permute-start.19 = (bf16[1024,512]{1,0:T(8,128)(2,1)}, bf16[1024,512]{1,0:T(8,128)(2,1)S(1)}, u32[]{:S(2)}, u32[]{:S(2)}) collective-permute-start(bf16[1024,512]{1,0:T(8,128)(2,1)} %bitcast.23), channel_id=1, source_target_pairs={{4,0},{8,4},{12,8},{0,12},{5,1},{9,5},{13,9},{1,13},{6,2},{10,6},{... | collective-permute-start | bytes 3145736 | tf_op jit(solution)/shard_map/ppermute | solution.py:194
  438.6 94.0 %collective-permute-start.53 = (bf16[1024,256]{1,0:T(8,128)(2,1)S(1)}, bf16[1024,256]{1,0:T(8,128)(2,1)S(1)}, u32[]{:S(2)}, u32[]{:S(2)}) collective-permute-start(bf16[1024,256]{1,0:T(8,128)(2,1)S(1)} %broadcast_select_fusion.5), channel_id=1, source_target_pairs={{0,4},{4,0},{8,12},{12,8},{1,5},{5,1},{9,13},{13,9},{2,6},{6,2},{1... | collective-permute-start | bytes 1572872 | tf_op jit(solution)/shard_map/ppermute | solution.py:196
  454.7 96.7 %collective-permute-start.50 = (bf16[1024,256]{1,0:T(8,128)(2,1)}, bf16[1024,256]{1,0:T(8,128)(2,1)}, u32[]{:S(2)}, u32[]{:S(2)}) collective-permute-start(bf16[1024,256]{1,0:T(8,128)(2,1)} %broadcast_select_fusion.6), channel_id=1, source_target_pairs={{0,4},{4,0},{8,12},{12,8},{1,5},{5,1},{9,13},{13,9},{2,6},{6,2},{1... | collective-permute-start | bytes 1572872 | tf_op jit(solution)/shard_map/ppermute | solution.py:196
  476.8 223.1 %collective-permute-start.14 = (bf16[1024,256]{1,0:T(8,128)(2,1)}, bf16[1024,256]{1,0:T(8,128)(2,1)}, u32[]{:S(2)}, u32[]{:S(2)}) collective-permute-start(bf16[1024,256]{1,0:T(8,128)(2,1)} %broadcast_select_fusion.7), channel_id=1, source_target_pairs={{0,4},{4,0},{8,12},{12,8},{1,5},{5,1},{9,13},{13,9},{2,6},{6,2},{1... | collective-permute-start | bytes 1572872 | tf_op jit(solution)/shard_map/ppermute | solution.py:196
  499.7 216.7 %collective-permute-start.8 = (bf16[1024,256]{1,0:T(8,128)(2,1)}, bf16[1024,256]{1,0:T(8,128)(2,1)}, u32[]{:S(2)}, u32[]{:S(2)}) collective-permute-start(bf16[1024,256]{1,0:T(8,128)(2,1)} %broadcast_select_fusion.8), channel_id=1, source_target_pairs={{0,4},{4,0},{8,12},{12,8},{1,5},{5,1},{9,13},{13,9},{2,6},{6,2},{1... | collective-permute-start | bytes 1572872 | tf_op jit(solution)/shard_map/ppermute | solution.py:196
  521.4 67.5 %collective-permute-start.44 = (bf16[1024,512]{1,0:T(8,128)(2,1)}, bf16[1024,512]{1,0:T(8,128)(2,1)}, u32[]{:S(2)}, u32[]{:S(2)}) collective-permute-start(bf16[1024,512]{1,0:T(8,128)(2,1)} %broadcast_select_fusion), channel_id=1, source_target_pairs={{0,4},{4,0},{8,12},{12,8},{1,5},{5,1},{9,13},{13,9},{2,6},{6,2},{1... | collective-permute-start | bytes 3145736 | tf_op jit(solution)/shard_map/ppermute | solution.py:196
  533.5 77.9 %collective-permute-start.38 = (bf16[1024,512]{1,0:T(8,128)(2,1)}, bf16[1024,512]{1,0:T(8,128)(2,1)}, u32[]{:S(2)}, u32[]{:S(2)}) collective-permute-start(bf16[1024,512]{1,0:T(8,128)(2,1)} %broadcast_select_fusion.1), channel_id=1, source_target_pairs={{0,4},{4,0},{8,12},{12,8},{1,5},{5,1},{9,13},{13,9},{2,6},{6,2},{1... | collective-permute-start | bytes 3145736 | tf_op jit(solution)/shard_map/ppermute | solution.py:196
  551.4 83.1 %collective-permute-start.32 = (bf16[1024,512]{1,0:T(8,128)(2,1)}, bf16[1024,512]{1,0:T(8,128)(2,1)}, u32[]{:S(2)}, u32[]{:S(2)}) collective-permute-start(bf16[1024,512]{1,0:T(8,128)(2,1)} %broadcast_select_fusion.2), channel_id=1, source_target_pairs={{0,4},{4,0},{8,12},{12,8},{1,5},{5,1},{9,13},{13,9},{2,6},{6,2},{1... | collective-permute-start | bytes 3145736 | tf_op jit(solution)/shard_map/ppermute | solution.py:196
  588.9 67.4 %collective-permute-start.26 = (bf16[1024,512]{1,0:T(8,128)(2,1)}, bf16[1024,512]{1,0:T(8,128)(2,1)}, u32[]{:S(2)}, u32[]{:S(2)}) collective-permute-start(bf16[1024,512]{1,0:T(8,128)(2,1)} %broadcast_select_fusion.3), channel_id=1, source_target_pairs={{0,4},{4,0},{8,12},{12,8},{1,5},{5,1},{9,13},{13,9},{2,6},{6,2},{1... | collective-permute-start | bytes 3145736 | tf_op jit(solution)/shard_map/ppermute | solution.py:196
  611.4 66.8 %collective-permute-start.20 = (bf16[1024,512]{1,0:T(8,128)(2,1)}, bf16[1024,512]{1,0:T(8,128)(2,1)}, u32[]{:S(2)}, u32[]{:S(2)}) collective-permute-start(bf16[1024,512]{1,0:T(8,128)(2,1)} %broadcast_select_fusion.4), channel_id=1, source_target_pairs={{0,4},{4,0},{8,12},{12,8},{1,5},{5,1},{9,13},{13,9},{2,6},{6,2},{1... | collective-permute-start | bytes 3145736 | tf_op jit(solution)/shard_map/ppermute | solution.py:196
  (74 other events, 2086.9 us)
Sparse Core Ops, SparseCore 0:
  39.8 246.9 all-gather.2

commit v2 on v0

v2 whole, which is shorter than its diff:
```python
import functools

import jax
import jax.numpy as jnp
from jax import lax
from jax.experimental import pallas as pl
from jax.experimental.pallas import tpu as pltpu
from jax.sharding import PartitionSpec as P

LANES = 128
VMEM_LIMIT = 52 * 2**20


def taking(us):
    return pl.CostEstimate(flops=int(us * 0.3 * 1.15e9), bytes_accessed=0, transcendentals=0)
WIDTHS = (4, 4, 4, 4, 4, 4, 2, 2)
ORDER = (
    "S0 A0 L0 S1",
    "S2 L1 O0 S3",
    "L2 O1 S4 W0.2",
    "L3 O2 S5 W1.2",
    "L4 X0 O3 S6",
    "W2.2 L5 X1 O4",
    "X2 W3.2 L6 O5",
    "X3 W4.2 O6 X4",
    "W5.2 L7 X5 O7",
    "X6 X7",
)
TOGETHER = {6: 2}


def plan(positions, rows):
    units = positions // LANES
    if sum(WIDTHS) == units and rows == 4:
        steps = " ".join(ORDER).split()
        order = [(step[0], step[1:]) for step in steps]
        return [part * LANES for part in WIDTHS], order, TOGETHER
    steps = [(kind, str(p)) for p in range(units) for kind in "SLX"]
    if rows == 4:
        steps = [(kind, str(p)) for p in range(units) for kind in "SLOX"]
    return [LANES] * units, steps[:2] + [("A", "0")] + steps[2:], {}


def select_kernel(slots, offset, layer_ref, to_ref, units_ref, perm_ref, *refs):
    outs, held = refs[-slots - 1 : -1], refs[-1]
    units = units_ref.shape[2]
    width = outs[0].shape[1]
    tile = 256 if width % 256 == 0 else width
    tiles = width // tile
    step = 1024 if units % 1024 == 0 else units

    @pl.loop(0, slots * tiles)
    def _(part):
        slot, start = part // tiles, pl.multiple_of((part % tiles) * tile, tile)
        wanted = perm_ref[to_ref[slot], :, pl.ds(pl.multiple_of(offset + start, LANES), tile)]

        total = None
        for at in range(0, units, step):
            index = lax.broadcasted_iota(jnp.int32, (step, tile), 0) + at
            hot = jnp.where(index == wanted, 1.0, 0.0).astype(jnp.bfloat16)
            term = jnp.dot(
                units_ref[0, :, at : at + step], hot, preferred_element_type=jnp.float32
            )
            total = term if total is None else total + term
        held[slot, :, pl.ds(start, tile)] = total.astype(jnp.bfloat16)

    for slot in range(slots):
        outs[slot][...] = held[slot]


def select_units(up_b, layer, perm, to, offset, width, after):
    slots, _, positions = perm.shape
    _, features, units = up_b.shape
    return pl.pallas_call(
        functools.partial(select_kernel, slots, offset),
        out_shape=[jax.ShapeDtypeStruct((features, width), jnp.bfloat16)] * slots,
        grid_spec=pltpu.PrefetchScalarGridSpec(
            num_scalar_prefetch=2,
            grid=(1,),
            in_specs=[
                pl.BlockSpec((1, features, units), lambda i, layer, to: (layer[0], 0, 0)),
                pl.BlockSpec((slots, 1, positions), lambda i, layer, to: (0, 0, 0)),
            ]
            + [pl.BlockSpec(memory_space=pl.ANY)] * len(after),
            out_specs=[pl.BlockSpec((features, width), lambda i, layer, to: (0, 0))] * slots,
            scratch_shapes=[
                pltpu.VMEM((slots, features, width), jnp.bfloat16),
            ],
        ),
        compiler_params=pltpu.CompilerParams(vmem_limit_bytes=VMEM_LIMIT),
        cost_estimate=taking(2 + width / 26),
        name="select_units",
    )(layer, to, up_b, perm, *after)


def place_kernel(slots, at_ref, *refs):
    out = refs[-1]
    for slot in range(slots):
        out[at_ref[slot]] = refs[slot][...]


def place(at, blocks, start, width, after):
    slots = len(blocks)
    features = blocks[0].shape[0]
    column = start // width
    return pl.pallas_call(
        functools.partial(place_kernel, slots),
        out_shape=jax.ShapeDtypeStruct((slots, features, width), jnp.bfloat16),
        grid_spec=pltpu.PrefetchScalarGridSpec(
            num_scalar_prefetch=1,
            grid=(1,),
            in_specs=[pl.BlockSpec((features, width), lambda i, at: (0, column))] * slots
            + [pl.BlockSpec(memory_space=pl.ANY)] * len(after),
            out_specs=pl.BlockSpec((slots, features, width), lambda i, at: (0, 0, 0)),
        ),
        compiler_params=pltpu.CompilerParams(vmem_limit_bytes=VMEM_LIMIT),
        cost_estimate=taking(1.6),
        name="place",
    )(at, *blocks, *after).reshape(slots * features, width)


def onward_kernel(odd_ref, ahead_ref, behind_ref, *refs):
    out = refs[-1]

    @pl.when(odd_ref[0] == 1)
    def _():
        out[...] = behind_ref[...]

    @pl.when(odd_ref[0] != 1)
    def _():
        out[...] = ahead_ref[...]


def onward(odd, ahead, behind, after):
    whole = pl.BlockSpec(ahead.shape, lambda i, odd: (0, 0))
    return pl.pallas_call(
        onward_kernel,
        out_shape=jax.ShapeDtypeStruct(ahead.shape, jnp.bfloat16),
        grid_spec=pltpu.PrefetchScalarGridSpec(
            num_scalar_prefetch=1,
            grid=(1,),
            in_specs=[whole, whole] + [pl.BlockSpec(memory_space=pl.ANY)] * len(after),
            out_specs=whole,
        ),
        compiler_params=pltpu.CompilerParams(vmem_limit_bytes=VMEM_LIMIT),
        cost_estimate=taking(1.6),
        name="onward",
    )(odd, ahead, behind, *after)


def pick_kernel(layer_ref, units_ref, *refs):
    refs[-1][...] = units_ref[0]


def pick(up_a, layer, after):
    _, features, units = up_a.shape
    tile = 256 if features % 256 == 0 else features
    return pl.pallas_call(
        pick_kernel,
        out_shape=jax.ShapeDtypeStruct((features, units), jnp.bfloat16),
        grid_spec=pltpu.PrefetchScalarGridSpec(
            num_scalar_prefetch=1,
            grid=(features // tile,),
            in_specs=[pl.BlockSpec((1, tile, units), lambda i, layer: (layer[0], i, 0))]
            + [pl.BlockSpec(memory_space=pl.ANY)] * len(after),
            out_specs=pl.BlockSpec((tile, units), lambda i, layer: (i, 0)),
        ),
        compiler_params=pltpu.CompilerParams(vmem_limit_bytes=VMEM_LIMIT),
        cost_estimate=taking(6.6),
        name="pick",
    )(layer, up_a, *after)


def product_kernel(blocks, joined, at_ref, *refs):
    lefts, rights = refs[: len(blocks)], refs[len(blocks) : 2 * len(blocks)]
    out = refs[-1]
    width = rights[0].shape[1]
    sums = {}
    for block, left, right in zip(blocks, lefts, rights):
        term = lax.dot_general(
            left[...], right[...], (((0,), (0,)), ((), ())), preferred_element_type=jnp.float32
        )
        start = block[1]
        sums[start] = sums[start] + term if start in sums else term
    for start, total in sums.items():
        columns = pl.ds(start, width)
        out[:, columns] = refs[2 * len(blocks)][:, columns] + total if joined else total


def product(left, at, rights, cost, offset, width, positions, joined, after):
    units = left.shape[1]
    block = rights[0][2].shape[0]
    tile = 512 if units % 512 == 0 else 256
    column = offset // width
    in_specs = [
        pl.BlockSpec((block, tile), lambda i, at, k=k: (at[k], i)) for k, _, _ in rights
    ] + [pl.BlockSpec(array.shape, lambda i, at: (0, 0)) for _, _, array in rights]
    operands = [left] * len(rights) + [array for _, _, array in rights]
    aliases = {}
    panel = pl.BlockSpec((tile, width), lambda i, at: (i, column))
    if cost is not None:
        operands.append(cost)
        in_specs.append(panel if joined else pl.BlockSpec(memory_space=pl.ANY))
        aliases = {len(operands): 0}
    operands += after
    in_specs += [pl.BlockSpec(memory_space=pl.ANY)] * len(after)
    return pl.pallas_call(
        functools.partial(product_kernel, [(k, start) for k, start, _ in rights], joined),
        out_shape=jax.ShapeDtypeStruct((units, positions), jnp.float32),
        grid_spec=pltpu.PrefetchScalarGridSpec(
            num_scalar_prefetch=1,
            grid=(units // tile,),
            in_specs=in_specs,
            out_specs=panel,
        ),
        input_output_aliases=aliases,
        compiler_params=pltpu.CompilerParams(vmem_limit_bytes=VMEM_LIMIT),
        cost_estimate=taking(11 + width / 48),
        name="product",
    )(at, *operands)


def exchange(sent, cols):
    back = [sent[0]]
    for s in range(1, cols):
        if cols & (cols - 1) == 0:
            pairs = [(i, i ^ s) for i in range(cols)]
        else:
            pairs = [(i, (i + s) % cols) for i in range(cols)]
        back.append(lax.ppermute(sent[s], "col", pairs))
    return back


def solution(mesh):
    rows, cols = mesh.shape["row"], mesh.shape["col"]
    ring = [[(i, (i + s) % rows) for i in range(rows)] for s in range(rows)]

    def shards(up_a, up_b, residual_perm, pair_index):
        r, c = lax.axis_index("row"), lax.axis_index("col")
        layer = pair_index
        positions = residual_perm.shape[0] // cols
        perm = residual_perm.reshape(cols, 1, positions)
        steps = jnp.arange(cols, dtype=jnp.int32)
        if cols & (cols - 1) == 0:
            to, come = c ^ steps, c ^ steps
        else:
            to, come = (c + steps) % cols, (c - steps) % cols
        at = (r - jnp.arange(rows, dtype=jnp.int32)) % rows
        odd = (r % 2).reshape(1).astype(jnp.int32)
        widths, order, together = plan(positions, rows)
        offsets = [sum(widths[:p]) for p in range(len(widths))]

        back, held = {}, {}
        left, cost, after = None, None, []
        for kind, number in order:
            if kind == "W":
                p, step = number.split(".")
                after = after + [held[int(p)][int(step)]]
                continue
            p = int(number)
            if kind == "S":
                members = range(p, p + together.get(p, 1))
                sent = select_units(
                    up_b, layer, perm, to, offsets[p], sum(widths[q] for q in members), after
                )
                came = exchange(sent, cols)
                for q in members:
                    back[q] = came, offsets[q] - offsets[p]
                last = sent[0]
            elif kind == "L":
                last = place(come, *back[p], widths[p], after)
                if rows == 4:
                    held[p] = [last, lax.ppermute(last, "row", ring[1]), None, lax.ppermute(last, "row", ring[3])]
                else:
                    held[p] = [last] + [lax.ppermute(last, "row", ring[s]) for s in range(1, rows)]
            elif kind == "O":
                last = onward(odd, held[p][1], held[p][3], after)
                held[p][2] = lax.ppermute(last, "row", [(0, 1), (1, 0), (2, 3), (3, 2)])
            elif kind == "A":
                last = pick(up_a, layer, after)
                left = lax.all_gather(last, "col", axis=0, tiled=True)
            else:
                rights = [(s, 0, array) for s, array in enumerate(held[p])]
                late = [array for array in after if array is not cost]
                cost = last = product(
                    left, at, rights, cost, offsets[p], widths[p], positions, False, late
                )
            after = [last]
        return cost

    placed = (
        P("groups", "col", "row"),
        P("groups", ("row", "col"), None),
        P("groups"),
        P("groups"),
    )
    return jax.shard_map(
        shards, mesh=mesh, in_specs=placed, out_specs=P(("groups", "row"), "col"), check_vma=False
    )
```

time: 894 us -> 566 us (0.63)
  waiting for transfers between devices: 496 us -> 138 us
  Pallas kernels: 0 us -> 339 us
  blocking collectives: 164 us -> 0 us
  matrix products: 120 us -> 0 us
  local copies, waits for them, and re-layouts: 95.2 us -> 11.1 us
  starting transfers between devices: 0.04 us -> 62.7 us
    all_gather x2 -> x1, waiting for transfers between devices: 496 us -> 0.01 us  [shards(): left = lax.all_gather(last, 'col', axis=0, tiled=True)]
    pallas_call x0 -> x32, Pallas kernels: none -> 339 us  [the longest x8 167 us: product(): pl.pallas_call(functools.partial(product_kernel, [(k, start) for k, start...]
    all_to_all x1 -> x0, blocking collectives: 164 us -> none  [shards(): lax.all_to_all(permuted, 'col', split_axis=1, concat_axis=0, tiled=True)]
    ppermute x0 -> x45, waiting for transfers between devices: none -> 138 us  [the longest x8 66.3 us: shards(): lax.ppermute(last, 'row', ring[3])]
    dot_general x1 -> x0, matrix products: 120 us -> none  [contract(): lax.dot_general(left, right, (((0,), (0,)), ((), ())), preferred_element_...]
    gather x2 -> x0, local copies, waits for them, and re-layouts: 69.8 us -> none  [shards(): permuted = jnp.take(right_units, residual_perm, axis=1)]
    ppermute x0 -> x45, starting transfers between devices: none -> 62.7 us  [the longest x8 34.7 us: shards(): lax.ppermute(last, 'row', ring[3])]
    dynamic_slice x3 -> x0, local copies, waits for them, and re-layouts: 24.6 us -> none  [the longest x2 18.1 us: shards(): right_units = lax.dynamic_index_in_dim(up_b, layer, 0, keepdims=False)]
  transfers between devices with their start and end apart: 2 -> 46, of which waited for: 2 -> 12; matrix products, arithmetic and copies ran while one was open for 10% -> 0% of each run, Pallas kernels for 0% -> 52%
where the time goes in v2:
time: 566 us
  Pallas kernels  339 us (60%)
  waiting for transfers between devices  138 us (24%)
  starting transfers between devices  62.7 us (11%)
  between operations  14.5 us (3%)
  local copies, waits for them, and re-layouts  11.1 us (2%)
    pallas_call x8, Pallas kernels, product(): pl.pallas_call(functools.partial(product_kernel, [(k, start) for k, start...  167 us
    pallas_call x7, Pallas kernels, select_units(): pl.pallas_call(functools.partial(select_kernel, slots, offset), out_shape...  144 us
    ppermute x8, waiting for transfers between devices, shards(): lax.ppermute(last, 'row', ring[3])  66.3 us
    ppermute x8, waiting for transfers between devices, shards(): lax.ppermute(last, 'row', ring[1])  56.6 us
    ppermute x8, starting transfers between devices, shards(): lax.ppermute(last, 'row', ring[3])  34.7 us
    ppermute x21, starting transfers between devices, exchange(): back.append(lax.ppermute(sent[s], 'col', pairs))  15.8 us
    ppermute x21, waiting for transfers between devices, exchange(): back.append(lax.ppermute(sent[s], 'col', pairs))  15 us
  transfers between devices with their start and end apart: 46, of which 12 were waited for; matrix products, arithmetic and copies ran while one was open for 0% of the time, Pallas kernels for 52%

profile of v2, /device:TPU:0, one launch (start us, length us, event | category | flops | bytes accessed | tf_op | source)
XLA Modules:
  0.0 565.6 jit_solution(11137845693134552158)
XLA Ops:
  8.0 20.3 %select_units.7 = (bf16[256,512]{1,0:T(8,128)(2,1)S(1)}, bf16[256,512]{1,0:T(8,128)(2,1)S(1)}, bf16[256,512]{1,0:T(8,128)(2,1)S(1)}, bf16[256,512]{1,0:T(8,128)(2,1)S(1)}) custom-call(s32[1]{0:T(128)S(6)} %copy.19.layer_ref, s32[4]{0:T(128)S(1)} %iota_xor_fusion.to_ref.at_ref, bf16[2,256,14336]{2,1,0:T(8,128)(2,1)} %units_ref.15, s32[4,1,3584]{2,1,0:T(1,128)S(1)} %bitcast.42), custom_call_target="tpu_custom_call" | custom-call | flops 7483846144 | tf_op jit(solution)/shard_map/select_units/pallas_call | solution.py:74
  55.7 22.1 %select_units.8 = (bf16[256,512]{1,0:T(8,128)(2,1)S(1)}, bf16[256,512]{1,0:T(8,128)(2,1)S(1)}, bf16[256,512]{1,0:T(8,128)(2,1)S(1)}, bf16[256,512]{1,0:T(8,128)(2,1)S(1)}) custom-call(s32[1]{0:T(128)S(6)} %copy.19.layer_ref, s32[4]{0:T(128)S(1)} %iota_xor_fusion.to_ref.at_ref, bf16[2,256,14336]{2,1,0:T(8,128)(2,1)} %units_ref.15, ...), custom_call_target="tpu_custom_call" | custom-call | flops 7483846144 | tf_op jit(solution)/shard_map/select_units/pallas_call | solution.py:74
  79.8 20.3 %select_units.9 = (bf16[256,512]{1,0:T(8,128)(2,1)S(1)}, bf16[256,512]{1,0:T(8,128)(2,1)S(1)}, bf16[256,512]{1,0:T(8,128)(2,1)S(1)}, bf16[256,512]{1,0:T(8,128)(2,1)S(1)}) custom-call(s32[1]{0:T(128)S(6)} %copy.19.layer_ref, s32[4]{0:T(128)S(1)} %iota_xor_fusion.to_ref.at_ref, bf16[2,256,14336]{2,1,0:T(8,128)(2,1)} %units_ref.15, ...), custom_call_target="tpu_custom_call" | custom-call | flops 7483846144 | tf_op jit(solution)/shard_map/select_units/pallas_call | solution.py:74
  113.0 20.3 %select_units.10 = (bf16[256,512]{1,0:T(8,128)(2,1)S(1)}, bf16[256,512]{1,0:T(8,128)(2,1)S(1)}, bf16[256,512]{1,0:T(8,128)(2,1)S(1)}, bf16[256,512]{1,0:T(8,128)(2,1)S(1)}) custom-call(s32[1]{0:T(128)S(6)} %copy.19.layer_ref, s32[4]{0:T(128)S(1)} %iota_xor_fusion.to_ref.at_ref, bf16[2,256,14336]{2,1,0:T(8,128)(2,1)} %units_ref.15, ...), custom_call_target="tpu_custom_call" | custom-call | flops 7483846144 | tf_op jit(solution)/shard_map/select_units/pallas_call | solution.py:74
  137.7 17.9 %collective-permute-start.23 = (bf16[1024,512]{1,0:T(8,128)(2,1)}, bf16[1024,512]{1,0:T(8,128)(2,1)S(1)}, u32[]{:S(2)}, u32[]{:S(2)}) collective-permute-start(bf16[1024,512]{1,0:T(8,128)(2,1)} %bitcast.23), channel_id=1, source_target_pairs={{0,12},{4,0},{8,4},{12,8},{1,13},{5,1},{9,5},{13,9},{2,14},{6,2},{... | collective-permute-start | bytes 3145736 | tf_op jit(solution)/shard_map/ppermute | solution.py:273
  158.4 20.3 %select_units.11 = (bf16[256,512]{1,0:T(8,128)(2,1)S(1)}, bf16[256,512]{1,0:T(8,128)(2,1)S(1)}, bf16[256,512]{1,0:T(8,128)(2,1)S(1)}, bf16[256,512]{1,0:T(8,128)(2,1)S(1)}) custom-call(s32[1]{0:T(128)S(6)} %copy.19.layer_ref, s32[4]{0:T(128)S(1)} %iota_xor_fusion.to_ref.at_ref, bf16[2,256,14336]{2,1,0:T(8,128)(2,1)} %units_ref.15, ...), custom_call_target="tpu_custom_call" | custom-call | flops 7483846144 | tf_op jit(solution)/shard_map/select_units/pallas_call | solution.py:74
  183.4 16.9 %collective-permute-done.22.ahead_ref.refs_5_ = bf16[1024,512]{1,0:T(8,128)(2,1)S(1)} collective-permute-done((bf16[1024,512]{1,0:T(8,128)(2,1)}, bf16[1024,512]{1,0:T(8,128)(2,1)S(1)}, u32[]{:S(2)}, u32[]{:S(2)}) %collective-permute-start.22) | collective-permute-done | bytes 1048608 | tf_op jit(solution)/shard_map/ppermute | solution.py:273
  202.1 18.9 %collective-permute-done.23.behind_ref.refs_7_ = bf16[1024,512]{1,0:T(8,128)(2,1)S(1)} collective-permute-done((bf16[1024,512]{1,0:T(8,128)(2,1)}, bf16[1024,512]{1,0:T(8,128)(2,1)S(1)}, u32[]{:S(2)}, u32[]{:S(2)}) %collective-permute-start.23) | collective-permute-done | bytes 1048608 | tf_op jit(solution)/shard_map/ppermute | solution.py:273
  227.0 20.3 %select_units.12 = (bf16[256,512]{1,0:T(8,128)(2,1)S(1)}, bf16[256,512]{1,0:T(8,128)(2,1)S(1)}, bf16[256,512]{1,0:T(8,128)(2,1)S(1)}, bf16[256,512]{1,0:T(8,128)(2,1)S(1)}) custom-call(s32[1]{0:T(128)S(6)} %copy.19.layer_ref, s32[4]{0:T(128)S(1)} %iota_xor_fusion.to_ref.at_ref, bf16[2,256,14336]{2,1,0:T(8,128)(2,1)} %units_ref.15, ...), custom_call_target="tpu_custom_call" | custom-call | flops 7483846144 | tf_op jit(solution)/shard_map/select_units/pallas_call | solution.py:74
  252.0 15.8 %collective-permute-done.17.ahead_ref.refs_5_ = bf16[1024,512]{1,0:T(8,128)(2,1)S(1)} collective-permute-done((bf16[1024,512]{1,0:T(8,128)(2,1)}, bf16[1024,512]{1,0:T(8,128)(2,1)S(1)}, u32[]{:S(2)}, u32[]{:S(2)}) %collective-permute-start.17) | collective-permute-done | bytes 1048608 | tf_op jit(solution)/shard_map/ppermute | solution.py:273
  268.0 22.2 %product.8.refs_0_.refs_8_ = f32[3584,3584]{1,0:T(8,128)} custom-call(s32[4]{0:T(128)S(1)} %and_select_fusion.at_ref, bf16[4096,3584]{1,0:T(8,128)(2,1)} %all-gather.2.cloned.1.call-done.refs_0_.refs_1_.refs_2_.refs_3_, bf16[4096,3584]{1,0:T(8,128)(2,1)} %all-gather.2.cloned.1.call-done.refs_0_.refs_1_.refs_2_.refs_3_, ...), custom_call_target="tpu_custom_call" | custom-call | flops 7474999808 | tf_op jit(solution)/shard_map/product/pallas_call | solution.py:207
  294.5 20.3 %select_units.13 = (bf16[256,512]{1,0:T(8,128)(2,1)S(1)}, bf16[256,512]{1,0:T(8,128)(2,1)S(1)}, bf16[256,512]{1,0:T(8,128)(2,1)S(1)}, bf16[256,512]{1,0:T(8,128)(2,1)S(1)}) custom-call(s32[1]{0:T(128)S(6)} %copy.19.layer_ref, s32[4]{0:T(128)S(1)} %iota_xor_fusion.to_ref.at_ref, bf16[2,256,14336]{2,1,0:T(8,128)(2,1)} %units_ref.15, ...), custom_call_target="tpu_custom_call" | custom-call | flops 7483846144 | tf_op jit(solution)/shard_map/select_units/pallas_call | solution.py:74
  322.3 13.1 %collective-permute-done.28.ahead_ref.refs_5_ = bf16[1024,512]{1,0:T(8,128)(2,1)} collective-permute-done((bf16[1024,512]{1,0:T(8,128)(2,1)}, bf16[1024,512]{1,0:T(8,128)(2,1)}, u32[]{:S(2)}, u32[]{:S(2)}) %collective-permute-start.28) | collective-permute-done | bytes 1048608 | tf_op jit(solution)/shard_map/ppermute | solution.py:273
  335.4 20.5 %collective-permute-done.29.behind_ref.refs_7_ = bf16[1024,512]{1,0:T(8,128)(2,1)} collective-permute-done((bf16[1024,512]{1,0:T(8,128)(2,1)}, bf16[1024,512]{1,0:T(8,128)(2,1)}, u32[]{:S(2)}, u32[]{:S(2)}) %collective-permute-start.29) | collective-permute-done | bytes 1048608 | tf_op jit(solution)/shard_map/ppermute | solution.py:273
  357.7 22.2 %product.9.refs_0_.refs_8_ = f32[3584,3584]{1,0:T(8,128)} custom-call(s32[4]{0:T(128)S(1)} %and_select_fusion.at_ref, bf16[4096,3584]{1,0:T(8,128)(2,1)} %all-gather.2.cloned.1.call-done.refs_0_.refs_1_.refs_2_.refs_3_, bf16[4096,3584]{1,0:T(8,128)(2,1)} %all-gather.2.cloned.1.call-done.refs_0_.refs_1_.refs_2_.refs_3_, ...), custom_call_target="tpu_custom_call", output_to_operand_aliasing={{}: (9, {})} | custom-call | flops 7474999808 | tf_op jit(solution)/shard_map/product/pallas_call | solution.py:207
  382.8 22.2 %product.10.refs_4_.refs_8_ = f32[3584,3584]{1,0:T(8,128)} custom-call(s32[4]{0:T(128)S(1)} %and_select_fusion.at_ref, bf16[4096,3584]{1,0:T(8,128)(2,1)} %all-gather.2.cloned.1.call-done.refs_0_.refs_1_.refs_2_.refs_3_, bf16[4096,3584]{1,0:T(8,128)(2,1)} %all-gather.2.cloned.1.call-done.refs_0_.refs_1_.refs_2_.refs_3_, ...), custom_call_target="tpu_custom_call", output_to_operand_aliasing={{}: (9, {})} | custom-call | flops 7474999808 | tf_op jit(solution)/shard_map/product/pallas_call | solution.py:207
  410.6 12.7 %collective-permute-done.37.behind_ref.refs_7_ = bf16[1024,512]{1,0:T(8,128)(2,1)} collective-permute-done((bf16[1024,512]{1,0:T(8,128)(2,1)}, bf16[1024,512]{1,0:T(8,128)(2,1)}, u32[]{:S(2)}, u32[]{:S(2)}) %collective-permute-start.37) | collective-permute-done | bytes 1048608 | tf_op jit(solution)/shard_map/ppermute | solution.py:273
  425.9 22.2 %product.11.refs_0_.refs_8_ = f32[3584,3584]{1,0:T(8,128)} custom-call(s32[4]{0:T(128)S(1)} %and_select_fusion.at_ref, bf16[4096,3584]{1,0:T(8,128)(2,1)} %all-gather.2.cloned.1.call-done.refs_0_.refs_1_.refs_2_.refs_3_, bf16[4096,3584]{1,0:T(8,128)(2,1)} %all-gather.2.cloned.1.call-done.refs_0_.refs_1_.refs_2_.refs_3_, ...), custom_call_target="tpu_custom_call", output_to_operand_aliasing={{}: (9, {})} | custom-call | flops 7474999808 | tf_op jit(solution)/shard_map/product/pallas_call | solution.py:207
  448.1 10.8 %collective-permute-done.38.ahead_ref.refs_5_ = bf16[1024,256]{1,0:T(8,128)(2,1)S(1)} collective-permute-done((bf16[1024,256]{1,0:T(8,128)(2,1)S(1)}, bf16[1024,256]{1,0:T(8,128)(2,1)S(1)}, u32[]{:S(2)}, u32[]{:S(2)}) %collective-permute-start.38) | collective-permute-done | bytes 524320 | tf_op jit(solution)/shard_map/ppermute | solution.py:273
  458.9 9.3 %collective-permute-done.39.behind_ref.refs_7_ = bf16[1024,256]{1,0:T(8,128)(2,1)S(1)} collective-permute-done((bf16[1024,256]{1,0:T(8,128)(2,1)S(1)}, bf16[1024,256]{1,0:T(8,128)(2,1)S(1)}, u32[]{:S(2)}, u32[]{:S(2)}) %collective-permute-start.39) | collective-permute-done | bytes 524320 | tf_op jit(solution)/shard_map/ppermute | solution.py:273
  469.0 22.2 %product.12.refs_4_.refs_8_ = f32[3584,3584]{1,0:T(8,128)} custom-call(s32[4]{0:T(128)S(1)} %and_select_fusion.at_ref, bf16[4096,3584]{1,0:T(8,128)(2,1)} %all-gather.2.cloned.1.call-done.refs_0_.refs_1_.refs_2_.refs_3_, bf16[4096,3584]{1,0:T(8,128)(2,1)} %all-gather.2.cloned.1.call-done.refs_0_.refs_1_.refs_2_.refs_3_, ...), custom_call_target="tpu_custom_call", output_to_operand_aliasing={{}: (9, {})} | custom-call | flops 7474999808 | tf_op jit(solution)/shard_map/product/pallas_call | solution.py:207
  496.9 22.2 %product.13.refs_0_.refs_8_ = f32[3584,3584]{1,0:T(8,128)} custom-call(s32[4]{0:T(128)S(1)} %and_select_fusion.at_ref, bf16[4096,3584]{1,0:T(8,128)(2,1)} %all-gather.2.cloned.1.call-done.refs_0_.refs_1_.refs_2_.refs_3_, bf16[4096,3584]{1,0:T(8,128)(2,1)} %all-gather.2.cloned.1.call-done.refs_0_.refs_1_.refs_2_.refs_3_, ...), custom_call_target="tpu_custom_call", output_to_operand_aliasing={{}: (9, {})} | custom-call | flops 7474999808 | tf_op jit(solution)/shard_map/product/pallas_call | solution.py:207
  525.0 16.9 %product.14.refs_8_ = f32[3584,3584]{1,0:T(8,128)} custom-call(s32[4]{0:T(128)S(1)} %and_select_fusion.at_ref, bf16[4096,3584]{1,0:T(8,128)(2,1)} %all-gather.2.cloned.1.call-done.refs_0_.refs_1_.refs_2_.refs_3_, bf16[4096,3584]{1,0:T(8,128)(2,1)} %all-gather.2.cloned.1.call-done.refs_0_.refs_1_.refs_2_.refs_3_, ...), custom_call_target="tpu_custom_call", output_to_operand_aliasing={{}: (9, {})} | custom-call | flops 5634999808 | tf_op jit(solution)/shard_map/product/pallas_call | solution.py:207
  542.0 16.8 %product.15 = f32[3584,3584]{1,0:T(8,128)} custom-call(s32[4]{0:T(128)S(1)} %and_select_fusion.at_ref, bf16[4096,3584]{1,0:T(8,128)(2,1)} %all-gather.2.cloned.1.call-done.refs_0_.refs_1_.refs_2_.refs_3_, bf16[4096,3584]{1,0:T(8,128)(2,1)} %all-gather.2.cloned.1.call-done.refs_0_.refs_1_.refs_2_.refs_3_, ...), custom_call_target="tpu_custom_call", output_to_operand_aliasing={{}: (9, {})} | custom-call | flops 5634999808 | tf_op jit(solution)/shard_map/product/pallas_call | solution.py:207
  (161 shorter events, 104.3 us)
Async XLA Ops:
  6.5 261.4 %all-gather.2.cloned.1.call-start = ((), (), s32[]{:S(2)}) async-start(), calls=%async_computation | async-start | bytes 36700160 | tf_op jit(solution)/shard_map/all_gather | solution.py:281
  51.8 56.8 %collective-permute-start.3 = (bf16[1024,512]{1,0:T(8,128)(2,1)}, bf16[1024,512]{1,0:T(8,128)(2,1)S(1)}, u32[]{:S(2)}, u32[]{:S(2)}) collective-permute-start(bf16[1024,512]{1,0:T(8,128)(2,1)} %bitcast.38), channel_id=1, source_target_pairs={{0,4},{4,8},{8,12},{12,0},{1,5},{5,9},{9,13},{13,1},{2,6},{6,10},{... | collective-permute-start | bytes 3145736 | tf_op jit(solution)/shard_map/ppermute | solution.py:273
  53.5 57.0 %collective-permute-start.4 = (bf16[1024,512]{1,0:T(8,128)(2,1)}, bf16[1024,512]{1,0:T(8,128)(2,1)}, u32[]{:S(2)}, u32[]{:S(2)}) collective-permute-start(bf16[1024,512]{1,0:T(8,128)(2,1)} %bitcast.39), channel_id=1, source_target_pairs={{0,12},{4,0},{8,4},{12,8},{1,13},{5,1},{9,5},{13,9},{2,14},{6,2},{... | collective-permute-start | bytes 3145736 | tf_op jit(solution)/shard_map/ppermute | solution.py:273
  104.9 50.7 %collective-permute-start.12 = (bf16[1024,512]{1,0:T(8,128)(2,1)}, bf16[1024,512]{1,0:T(8,128)(2,1)}, u32[]{:S(2)}, u32[]{:S(2)}) collective-permute-start(bf16[1024,512]{1,0:T(8,128)(2,1)} %bitcast.19), channel_id=1, source_target_pairs={{0,12},{4,0},{8,4},{12,8},{1,13},{5,1},{9,5},{13,9},{2,14},{6,2},{... | collective-permute-start | bytes 3145736 | tf_op jit(solution)/shard_map/ppermute | solution.py:273
  112.1 67.7 %collective-permute-start.16 = (bf16[1024,512]{1,0:T(8,128)(2,1)S(1)}, bf16[1024,512]{1,0:T(8,128)(2,1)S(1)}, u32[]{:S(2)}, u32[]{:S(2)}) collective-permute-start(bf16[1024,512]{1,0:T(8,128)(2,1)S(1)} %onward.8.refs_0_), channel_id=1, source_target_pairs={{0,4},{4,0},{8,12},{12,8},{1,5},{5,1},{9,13},{13,9},{2,6},{6,2},{1... | collective-permute-start | bytes 3145736 | tf_op jit(solution)/shard_map/ppermute | solution.py:278
  136.8 63.5 %collective-permute-start.22 = (bf16[1024,512]{1,0:T(8,128)(2,1)}, bf16[1024,512]{1,0:T(8,128)(2,1)S(1)}, u32[]{:S(2)}, u32[]{:S(2)}) collective-permute-start(bf16[1024,512]{1,0:T(8,128)(2,1)} %bitcast.22), channel_id=1, source_target_pairs={{0,4},{4,8},{8,12},{12,0},{1,5},{5,9},{9,13},{13,1},{2,6},{6,10},{... | collective-permute-start | bytes 3145736 | tf_op jit(solution)/shard_map/ppermute | solution.py:273
  137.7 83.3 %collective-permute-start.23 = (bf16[1024,512]{1,0:T(8,128)(2,1)}, bf16[1024,512]{1,0:T(8,128)(2,1)S(1)}, u32[]{:S(2)}, u32[]{:S(2)}) collective-permute-start(bf16[1024,512]{1,0:T(8,128)(2,1)} %bitcast.23), channel_id=1, source_target_pairs={{0,12},{4,0},{8,4},{12,8},{1,13},{5,1},{9,5},{13,9},{2,14},{6,2},{... | collective-permute-start | bytes 3145736 | tf_op jit(solution)/shard_map/ppermute | solution.py:273
  178.7 69.0 %collective-permute-start.24 = (bf16[1024,512]{1,0:T(8,128)(2,1)}, bf16[1024,512]{1,0:T(8,128)(2,1)S(1)}, u32[]{:S(2)}, u32[]{:S(2)}) collective-permute-start(bf16[1024,512]{1,0:T(8,128)(2,1)} %copy-done.15), channel_id=1, source_target_pairs={{0,4},{4,0},{8,12},{12,8},{1,5},{5,1},{9,13},{13,9},{2,6},{6,2},{1... | collective-permute-start | bytes 3145736 | tf_op jit(solution)/shard_map/ppermute | solution.py:278
  182.4 85.4 %collective-permute-start.17 = (bf16[1024,512]{1,0:T(8,128)(2,1)}, bf16[1024,512]{1,0:T(8,128)(2,1)S(1)}, u32[]{:S(2)}, u32[]{:S(2)}) collective-permute-start(bf16[1024,512]{1,0:T(8,128)(2,1)} %bitcast.26), channel_id=1, source_target_pairs={{0,4},{4,8},{8,12},{12,0},{1,5},{5,9},{9,13},{13,1},{2,6},{6,10},{... | collective-permute-start | bytes 3145736 | tf_op jit(solution)/shard_map/ppermute | solution.py:273
  200.4 46.9 %collective-permute-start.20 = (bf16[256,512]{1,0:T(8,128)(2,1)S(1)}, bf16[256,512]{1,0:T(8,128)(2,1)S(1)}, u32[]{:S(2)}, u32[]{:S(2)}) collective-permute-start(bf16[256,512]{1,0:T(8,128)(2,1)S(1)} %get-tuple-element.51), channel_id=1, source_target_pairs={{0,2},{1,3},{2,0},{3,1},{4,6},{5,7},{6,4},{7,5},{8,10},{9,11},{10,... | collective-permute-start | bytes 786440 | tf_op jit(solution)/shard_map/ppermute | solution.py:230
  224.7 65.5 %collective-permute-start.18 = (bf16[1024,512]{1,0:T(8,128)(2,1)}, bf16[1024,512]{1,0:T(8,128)(2,1)}, u32[]{:S(2)}, u32[]{:S(2)}) collective-permute-start(bf16[1024,512]{1,0:T(8,128)(2,1)} %bitcast.28), channel_id=1, source_target_pairs={{0,12},{4,0},{8,4},{12,8},{1,13},{5,1},{9,5},{13,9},{2,14},{6,2},{... | collective-permute-start | bytes 3145736 | tf_op jit(solution)/shard_map/ppermute | solution.py:273
  247.3 69.6 %collective-permute-start.33 = (bf16[1024,512]{1,0:T(8,128)(2,1)}, bf16[1024,512]{1,0:T(8,128)(2,1)}, u32[]{:S(2)}, u32[]{:S(2)}) collective-permute-start(bf16[1024,512]{1,0:T(8,128)(2,1)} %copy-done.13), channel_id=1, source_target_pairs={{0,4},{4,0},{8,12},{12,8},{1,5},{5,1},{9,13},{13,9},{2,6},{6,2},{1... | collective-permute-start | bytes 3145736 | tf_op jit(solution)/shard_map/ppermute | solution.py:278
  247.4 47.1 %collective-permute-start.30 = (bf16[256,512]{1,0:T(8,128)(2,1)S(1)}, bf16[256,512]{1,0:T(8,128)(2,1)S(1)}, u32[]{:S(2)}, u32[]{:S(2)}) collective-permute-start(bf16[256,512]{1,0:T(8,128)(2,1)S(1)} %get-tuple-element.58), channel_id=1, source_target_pairs={{0,1},{1,0},{2,3},{3,2},{4,5},{5,4},{6,7},{7,6},{8,9},{9,8},{10,11... | collective-permute-start | bytes 786440 | tf_op jit(solution)/shard_map/ppermute | solution.py:230
  250.2 85.2 %collective-permute-start.28 = (bf16[1024,512]{1,0:T(8,128)(2,1)}, bf16[1024,512]{1,0:T(8,128)(2,1)}, u32[]{:S(2)}, u32[]{:S(2)}) collective-permute-start(bf16[1024,512]{1,0:T(8,128)(2,1)} %bitcast.10), channel_id=1, source_target_pairs={{0,4},{4,8},{8,12},{12,0},{1,5},{5,9},{9,13},{13,1},{2,6},{6,10},{... | collective-permute-start | bytes 3145736 | tf_op jit(solution)/shard_map/ppermute | solution.py:273
  267.8 88.1 %collective-permute-start.29 = (bf16[1024,512]{1,0:T(8,128)(2,1)}, bf16[1024,512]{1,0:T(8,128)(2,1)}, u32[]{:S(2)}, u32[]{:S(2)}) collective-permute-start(bf16[1024,512]{1,0:T(8,128)(2,1)} %bitcast.11), channel_id=1, source_target_pairs={{0,12},{4,0},{8,4},{12,8},{1,13},{5,1},{9,5},{13,9},{2,14},{6,2},{... | collective-permute-start | bytes 3145736 | tf_op jit(solution)/shard_map/ppermute | solution.py:273
  314.8 90.3 %collective-permute-start.35 = (bf16[1024,512]{1,0:T(8,128)(2,1)}, bf16[1024,512]{1,0:T(8,128)(2,1)S(1)}, u32[]{:S(2)}, u32[]{:S(2)}) collective-permute-start(bf16[1024,512]{1,0:T(8,128)(2,1)} %copy-done.14), channel_id=1, source_target_pairs={{0,4},{4,0},{8,12},{12,8},{1,5},{5,1},{9,13},{13,9},{2,6},{6,2},{1... | collective-permute-start | bytes 3145736 | tf_op jit(solution)/shard_map/ppermute | solution.py:278
  318.5 92.1 %collective-permute-start.36 = (bf16[1024,512]{1,0:T(8,128)(2,1)}, bf16[1024,512]{1,0:T(8,128)(2,1)}, u32[]{:S(2)}, u32[]{:S(2)}) collective-permute-start(bf16[1024,512]{1,0:T(8,128)(2,1)} %bitcast.14), channel_id=1, source_target_pairs={{0,4},{4,8},{8,12},{12,0},{1,5},{5,9},{9,13},{13,1},{2,6},{6,10},{... | collective-permute-start | bytes 3145736 | tf_op jit(solution)/shard_map/ppermute | solution.py:273
  318.5 104.8 %collective-permute-start.37 = (bf16[1024,512]{1,0:T(8,128)(2,1)}, bf16[1024,512]{1,0:T(8,128)(2,1)}, u32[]{:S(2)}, u32[]{:S(2)}) collective-permute-start(bf16[1024,512]{1,0:T(8,128)(2,1)} %bitcast.15), channel_id=1, source_target_pairs={{0,12},{4,0},{8,4},{12,8},{1,13},{5,1},{9,5},{13,9},{2,14},{6,2},{... | collective-permute-start | bytes 3145736 | tf_op jit(solution)/shard_map/ppermute | solution.py:273
  335.4 46.4 %collective-permute-start.25 = (bf16[256,512]{1,0:T(8,128)(2,1)S(1)}, bf16[256,512]{1,0:T(8,128)(2,1)S(1)}, u32[]{:S(2)}, u32[]{:S(2)}) collective-permute-start(bf16[256,512]{1,0:T(8,128)(2,1)S(1)} %get-tuple-element.55), channel_id=1, source_target_pairs={{0,1},{1,0},{2,3},{3,2},{4,5},{5,4},{6,7},{7,6},{8,9},{9,8},{10,11... | collective-permute-start | bytes 786440 | tf_op jit(solution)/shard_map/ppermute | solution.py:230
  381.9 66.2 %collective-permute-start.34 = (bf16[1024,512]{1,0:T(8,128)(2,1)S(1)}, bf16[1024,512]{1,0:T(8,128)(2,1)S(1)}, u32[]{:S(2)}, u32[]{:S(2)}) collective-permute-start(bf16[1024,512]{1,0:T(8,128)(2,1)S(1)} %onward.12.refs_9_), channel_id=1, source_target_pairs={{0,4},{4,0},{8,12},{12,8},{1,5},{5,1},{9,13},{13,9},{2,6},{6,2},{1... | collective-permute-start | bytes 3145736 | tf_op jit(solution)/shard_map/ppermute | solution.py:278
  406.7 52.2 %collective-permute-start.38 = (bf16[1024,256]{1,0:T(8,128)(2,1)S(1)}, bf16[1024,256]{1,0:T(8,128)(2,1)S(1)}, u32[]{:S(2)}, u32[]{:S(2)}) collective-permute-start(bf16[1024,256]{1,0:T(8,128)(2,1)S(1)} %bitcast.34), channel_id=1, source_target_pairs={{0,4},{4,8},{8,12},{12,0},{1,5},{5,9},{9,13},{13,1},{2,6},{6,10},{... | collective-permute-start | bytes 1572872 | tf_op jit(solution)/shard_map/ppermute | solution.py:273
  408.0 60.2 %collective-permute-start.39 = (bf16[1024,256]{1,0:T(8,128)(2,1)S(1)}, bf16[1024,256]{1,0:T(8,128)(2,1)S(1)}, u32[]{:S(2)}, u32[]{:S(2)}) collective-permute-start(bf16[1024,256]{1,0:T(8,128)(2,1)S(1)} %bitcast.35), channel_id=1, source_target_pairs={{0,12},{4,0},{8,4},{12,8},{1,13},{5,1},{9,5},{13,9},{2,14},{6,2},{... | collective-permute-start | bytes 1572872 | tf_op jit(solution)/shard_map/ppermute | solution.py:273
  424.9 66.3 %collective-permute-start.40 = (bf16[1024,512]{1,0:T(8,128)(2,1)S(1)}, bf16[1024,512]{1,0:T(8,128)(2,1)S(1)}, u32[]{:S(2)}, u32[]{:S(2)}) collective-permute-start(bf16[1024,512]{1,0:T(8,128)(2,1)S(1)} %onward.13.refs_9_), channel_id=1, source_target_pairs={{0,4},{4,0},{8,12},{12,8},{1,5},{5,1},{9,13},{13,9},{2,6},{6,2},{1... | collective-permute-start | bytes 3145736 | tf_op jit(solution)/shard_map/ppermute | solution.py:278
  469.0 55.2 %collective-permute-start.44 = (bf16[1024,256]{1,0:T(8,128)(2,1)}, bf16[1024,256]{1,0:T(8,128)(2,1)}, u32[]{:S(2)}, u32[]{:S(2)}) collective-permute-start(bf16[1024,256]{1,0:T(8,128)(2,1)} %onward.14.refs_9_), channel_id=1, source_target_pairs={{0,4},{4,0},{8,12},{12,8},{1,5},{5,1},{9,13},{13,9},{2,6},{6,2},{1... | collective-permute-start | bytes 1572872 | tf_op jit(solution)/shard_map/ppermute | solution.py:278
  (51 other events, 1025.0 us)
Sparse Core Ops, SparseCore 0:
  35.0 225.6 all-gather.1

commit v3 on v2

--- a/solution.py
+++ b/solution.py
@@ -190,7 +190,7 @@
 def product(left, at, rights, cost, offset, width, positions, joined, after):
     units = left.shape[1]
     block = rights[0][2].shape[0]
-    tile = 512 if units % 512 == 0 else 256
+    tile = 896 if units % 896 == 0 else 256
     column = offset // width
     in_specs = [
         pl.BlockSpec((block, tile), lambda i, at, k=k: (at[k], i)) for k, _, _ in rights

time: 566 us -> 572 us (1.011); the launches traced: 566 us -> 564 us
  transfers between devices with their start and end apart: 46 -> 46, of which waited for: 12 -> 12; matrix products, arithmetic and copies ran while one was open for 0% -> 0% of each run, Pallas kernels for 52% -> 53%
where the time goes in v3:
time: 572 us; the launch traced here: 564 us
  Pallas kernels  339 us (59%)
  waiting for transfers between devices  136 us (24%)
  starting transfers between devices  63.2 us (11%)
  between operations  14.9 us (3%)
  local copies, waits for them, and re-layouts  11.1 us (2%)
    pallas_call x8, Pallas kernels, product(): pl.pallas_call(functools.partial(product_kernel, [(k, start) for k, start...  167 us
    pallas_call x7, Pallas kernels, select_units(): pl.pallas_call(functools.partial(select_kernel, slots, offset), out_shape...  144 us
    ppermute x8, waiting for transfers between devices, shards(): lax.ppermute(last, 'row', ring[3])  64.8 us
    ppermute x8, waiting for transfers between devices, shards(): lax.ppermute(last, 'row', ring[1])  55.8 us
    ppermute x8, starting transfers between devices, shards(): lax.ppermute(last, 'row', ring[3])  35.3 us
    ppermute x21, starting transfers between devices, exchange(): back.append(lax.ppermute(sent[s], 'col', pairs))  15.8 us
    ppermute x21, waiting for transfers between devices, exchange(): back.append(lax.ppermute(sent[s], 'col', pairs))  15 us
  transfers between devices with their start and end apart: 46, of which 12 were waited for; matrix products, arithmetic and copies ran while one was open for 0% of the time, Pallas kernels for 53%

profile of v3, /device:TPU:0, one launch (start us, length us, event | category | flops | bytes accessed | tf_op | source)
XLA Modules:
  0.0 563.9 jit_solution(771403432981804296)
XLA Ops:
  8.0 20.3 %select_units.7 = (bf16[256,512]{1,0:T(8,128)(2,1)S(1)}, bf16[256,512]{1,0:T(8,128)(2,1)S(1)}, bf16[256,512]{1,0:T(8,128)(2,1)S(1)}, bf16[256,512]{1,0:T(8,128)(2,1)S(1)}) custom-call(s32[1]{0:T(128)S(6)} %copy.19.layer_ref, s32[4]{0:T(128)S(1)} %iota_xor_fusion.to_ref.at_ref, bf16[2,256,14336]{2,1,0:T(8,128)(2,1)} %units_ref.15, s32[4,1,3584]{2,1,0:T(1,128)S(1)} %bitcast.42), custom_call_target="tpu_custom_call" | custom-call | flops 7483846144 | tf_op jit(solution)/shard_map/select_units/pallas_call | solution.py:74
  55.7 22.1 %select_units.8 = (bf16[256,512]{1,0:T(8,128)(2,1)S(1)}, bf16[256,512]{1,0:T(8,128)(2,1)S(1)}, bf16[256,512]{1,0:T(8,128)(2,1)S(1)}, bf16[256,512]{1,0:T(8,128)(2,1)S(1)}) custom-call(s32[1]{0:T(128)S(6)} %copy.19.layer_ref, s32[4]{0:T(128)S(1)} %iota_xor_fusion.to_ref.at_ref, bf16[2,256,14336]{2,1,0:T(8,128)(2,1)} %units_ref.15, ...), custom_call_target="tpu_custom_call" | custom-call | flops 7483846144 | tf_op jit(solution)/shard_map/select_units/pallas_call | solution.py:74
  79.8 20.3 %select_units.9 = (bf16[256,512]{1,0:T(8,128)(2,1)S(1)}, bf16[256,512]{1,0:T(8,128)(2,1)S(1)}, bf16[256,512]{1,0:T(8,128)(2,1)S(1)}, bf16[256,512]{1,0:T(8,128)(2,1)S(1)}) custom-call(s32[1]{0:T(128)S(6)} %copy.19.layer_ref, s32[4]{0:T(128)S(1)} %iota_xor_fusion.to_ref.at_ref, bf16[2,256,14336]{2,1,0:T(8,128)(2,1)} %units_ref.15, ...), custom_call_target="tpu_custom_call" | custom-call | flops 7483846144 | tf_op jit(solution)/shard_map/select_units/pallas_call | solution.py:74
  113.0 20.3 %select_units.10 = (bf16[256,512]{1,0:T(8,128)(2,1)S(1)}, bf16[256,512]{1,0:T(8,128)(2,1)S(1)}, bf16[256,512]{1,0:T(8,128)(2,1)S(1)}, bf16[256,512]{1,0:T(8,128)(2,1)S(1)}) custom-call(s32[1]{0:T(128)S(6)} %copy.19.layer_ref, s32[4]{0:T(128)S(1)} %iota_xor_fusion.to_ref.at_ref, bf16[2,256,14336]{2,1,0:T(8,128)(2,1)} %units_ref.15, ...), custom_call_target="tpu_custom_call" | custom-call | flops 7483846144 | tf_op jit(solution)/shard_map/select_units/pallas_call | solution.py:74
  137.7 17.9 %collective-permute-start.23 = (bf16[1024,512]{1,0:T(8,128)(2,1)}, bf16[1024,512]{1,0:T(8,128)(2,1)S(1)}, u32[]{:S(2)}, u32[]{:S(2)}) collective-permute-start(bf16[1024,512]{1,0:T(8,128)(2,1)} %bitcast.23), channel_id=1, source_target_pairs={{0,12},{4,0},{8,4},{12,8},{1,13},{5,1},{9,5},{13,9},{2,14},{6,2},{... | collective-permute-start | bytes 3145736 | tf_op jit(solution)/shard_map/ppermute | solution.py:273
  158.4 20.3 %select_units.11 = (bf16[256,512]{1,0:T(8,128)(2,1)S(1)}, bf16[256,512]{1,0:T(8,128)(2,1)S(1)}, bf16[256,512]{1,0:T(8,128)(2,1)S(1)}, bf16[256,512]{1,0:T(8,128)(2,1)S(1)}) custom-call(s32[1]{0:T(128)S(6)} %copy.19.layer_ref, s32[4]{0:T(128)S(1)} %iota_xor_fusion.to_ref.at_ref, bf16[2,256,14336]{2,1,0:T(8,128)(2,1)} %units_ref.15, ...), custom_call_target="tpu_custom_call" | custom-call | flops 7483846144 | tf_op jit(solution)/shard_map/select_units/pallas_call | solution.py:74
  183.4 16.9 %collective-permute-done.22.ahead_ref.refs_5_ = bf16[1024,512]{1,0:T(8,128)(2,1)S(1)} collective-permute-done((bf16[1024,512]{1,0:T(8,128)(2,1)}, bf16[1024,512]{1,0:T(8,128)(2,1)S(1)}, u32[]{:S(2)}, u32[]{:S(2)}) %collective-permute-start.22) | collective-permute-done | bytes 1048608 | tf_op jit(solution)/shard_map/ppermute | solution.py:273
  202.1 18.9 %collective-permute-done.23.behind_ref.refs_7_ = bf16[1024,512]{1,0:T(8,128)(2,1)S(1)} collective-permute-done((bf16[1024,512]{1,0:T(8,128)(2,1)}, bf16[1024,512]{1,0:T(8,128)(2,1)S(1)}, u32[]{:S(2)}, u32[]{:S(2)}) %collective-permute-start.23) | collective-permute-done | bytes 1048608 | tf_op jit(solution)/shard_map/ppermute | solution.py:273
  227.0 20.3 %select_units.12 = (bf16[256,512]{1,0:T(8,128)(2,1)S(1)}, bf16[256,512]{1,0:T(8,128)(2,1)S(1)}, bf16[256,512]{1,0:T(8,128)(2,1)S(1)}, bf16[256,512]{1,0:T(8,128)(2,1)S(1)}) custom-call(s32[1]{0:T(128)S(6)} %copy.19.layer_ref, s32[4]{0:T(128)S(1)} %iota_xor_fusion.to_ref.at_ref, bf16[2,256,14336]{2,1,0:T(8,128)(2,1)} %units_ref.15, ...), custom_call_target="tpu_custom_call" | custom-call | flops 7483846144 | tf_op jit(solution)/shard_map/select_units/pallas_call | solution.py:74
  252.0 15.8 %collective-permute-done.17.ahead_ref.refs_5_ = bf16[1024,512]{1,0:T(8,128)(2,1)S(1)} collective-permute-done((bf16[1024,512]{1,0:T(8,128)(2,1)}, bf16[1024,512]{1,0:T(8,128)(2,1)S(1)}, u32[]{:S(2)}, u32[]{:S(2)}) %collective-permute-start.17) | collective-permute-done | bytes 1048608 | tf_op jit(solution)/shard_map/ppermute | solution.py:273
  268.0 22.5 %product.8.refs_0_.refs_8_ = f32[3584,3584]{1,0:T(8,128)} custom-call(s32[4]{0:T(128)S(1)} %and_select_fusion.at_ref, bf16[4096,3584]{1,0:T(8,128)(2,1)} %all-gather.2.cloned.1.call-done.refs_0_.refs_1_.refs_2_.refs_3_, bf16[4096,3584]{1,0:T(8,128)(2,1)} %all-gather.2.cloned.1.call-done.refs_0_.refs_1_.refs_2_.refs_3_, ...), custom_call_target="tpu_custom_call" | custom-call | flops 7474999808 | tf_op jit(solution)/shard_map/product/pallas_call | solution.py:207
  294.8 20.3 %select_units.13 = (bf16[256,512]{1,0:T(8,128)(2,1)S(1)}, bf16[256,512]{1,0:T(8,128)(2,1)S(1)}, bf16[256,512]{1,0:T(8,128)(2,1)S(1)}, bf16[256,512]{1,0:T(8,128)(2,1)S(1)}) custom-call(s32[1]{0:T(128)S(6)} %copy.19.layer_ref, s32[4]{0:T(128)S(1)} %iota_xor_fusion.to_ref.at_ref, bf16[2,256,14336]{2,1,0:T(8,128)(2,1)} %units_ref.15, ...), custom_call_target="tpu_custom_call" | custom-call | flops 7483846144 | tf_op jit(solution)/shard_map/select_units/pallas_call | solution.py:74
  322.8 12.6 %collective-permute-done.28.ahead_ref.refs_5_ = bf16[1024,512]{1,0:T(8,128)(2,1)} collective-permute-done((bf16[1024,512]{1,0:T(8,128)(2,1)}, bf16[1024,512]{1,0:T(8,128)(2,1)}, u32[]{:S(2)}, u32[]{:S(2)}) %collective-permute-start.28) | collective-permute-done | bytes 1048608 | tf_op jit(solution)/shard_map/ppermute | solution.py:273
  335.4 20.5 %collective-permute-done.29.behind_ref.refs_7_ = bf16[1024,512]{1,0:T(8,128)(2,1)} collective-permute-done((bf16[1024,512]{1,0:T(8,128)(2,1)}, bf16[1024,512]{1,0:T(8,128)(2,1)}, u32[]{:S(2)}, u32[]{:S(2)}) %collective-permute-start.29) | collective-permute-done | bytes 1048608 | tf_op jit(solution)/shard_map/ppermute | solution.py:273
  357.7 22.5 %product.9.refs_0_.refs_8_ = f32[3584,3584]{1,0:T(8,128)} custom-call(s32[4]{0:T(128)S(1)} %and_select_fusion.at_ref, bf16[4096,3584]{1,0:T(8,128)(2,1)} %all-gather.2.cloned.1.call-done.refs_0_.refs_1_.refs_2_.refs_3_, bf16[4096,3584]{1,0:T(8,128)(2,1)} %all-gather.2.cloned.1.call-done.refs_0_.refs_1_.refs_2_.refs_3_, ...), custom_call_target="tpu_custom_call", output_to_operand_aliasing={{}: (9, {})} | custom-call | flops 7474999808 | tf_op jit(solution)/shard_map/product/pallas_call | solution.py:207
  383.0 22.6 %product.10.refs_4_.refs_8_ = f32[3584,3584]{1,0:T(8,128)} custom-call(s32[4]{0:T(128)S(1)} %and_select_fusion.at_ref, bf16[4096,3584]{1,0:T(8,128)(2,1)} %all-gather.2.cloned.1.call-done.refs_0_.refs_1_.refs_2_.refs_3_, bf16[4096,3584]{1,0:T(8,128)(2,1)} %all-gather.2.cloned.1.call-done.refs_0_.refs_1_.refs_2_.refs_3_, ...), custom_call_target="tpu_custom_call", output_to_operand_aliasing={{}: (9, {})} | custom-call | flops 7474999808 | tf_op jit(solution)/shard_map/product/pallas_call | solution.py:207
  411.1 12.3 %collective-permute-done.37.behind_ref.refs_7_ = bf16[1024,512]{1,0:T(8,128)(2,1)} collective-permute-done((bf16[1024,512]{1,0:T(8,128)(2,1)}, bf16[1024,512]{1,0:T(8,128)(2,1)}, u32[]{:S(2)}, u32[]{:S(2)}) %collective-permute-start.37) | collective-permute-done | bytes 1048608 | tf_op jit(solution)/shard_map/ppermute | solution.py:273
  425.9 22.6 %product.11.refs_0_.refs_8_ = f32[3584,3584]{1,0:T(8,128)} custom-call(s32[4]{0:T(128)S(1)} %and_select_fusion.at_ref, bf16[4096,3584]{1,0:T(8,128)(2,1)} %all-gather.2.cloned.1.call-done.refs_0_.refs_1_.refs_2_.refs_3_, bf16[4096,3584]{1,0:T(8,128)(2,1)} %all-gather.2.cloned.1.call-done.refs_0_.refs_1_.refs_2_.refs_3_, ...), custom_call_target="tpu_custom_call", output_to_operand_aliasing={{}: (9, {})} | custom-call | flops 7474999808 | tf_op jit(solution)/shard_map/product/pallas_call | solution.py:207
  448.5 10.4 %collective-permute-done.38.ahead_ref.refs_5_ = bf16[1024,256]{1,0:T(8,128)(2,1)S(1)} collective-permute-done((bf16[1024,256]{1,0:T(8,128)(2,1)S(1)}, bf16[1024,256]{1,0:T(8,128)(2,1)S(1)}, u32[]{:S(2)}, u32[]{:S(2)}) %collective-permute-start.38) | collective-permute-done | bytes 524320 | tf_op jit(solution)/shard_map/ppermute | solution.py:273
  458.9 9.3 %collective-permute-done.39.behind_ref.refs_7_ = bf16[1024,256]{1,0:T(8,128)(2,1)S(1)} collective-permute-done((bf16[1024,256]{1,0:T(8,128)(2,1)S(1)}, bf16[1024,256]{1,0:T(8,128)(2,1)S(1)}, u32[]{:S(2)}, u32[]{:S(2)}) %collective-permute-start.39) | collective-permute-done | bytes 524320 | tf_op jit(solution)/shard_map/ppermute | solution.py:273
  469.0 22.5 %product.12.refs_4_.refs_8_ = f32[3584,3584]{1,0:T(8,128)} custom-call(s32[4]{0:T(128)S(1)} %and_select_fusion.at_ref, bf16[4096,3584]{1,0:T(8,128)(2,1)} %all-gather.2.cloned.1.call-done.refs_0_.refs_1_.refs_2_.refs_3_, bf16[4096,3584]{1,0:T(8,128)(2,1)} %all-gather.2.cloned.1.call-done.refs_0_.refs_1_.refs_2_.refs_3_, ...), custom_call_target="tpu_custom_call", output_to_operand_aliasing={{}: (9, {})} | custom-call | flops 7474999808 | tf_op jit(solution)/shard_map/product/pallas_call | solution.py:207
  497.5 22.7 %product.13.refs_0_.refs_8_ = f32[3584,3584]{1,0:T(8,128)} custom-call(s32[4]{0:T(128)S(1)} %and_select_fusion.at_ref, bf16[4096,3584]{1,0:T(8,128)(2,1)} %all-gather.2.cloned.1.call-done.refs_0_.refs_1_.refs_2_.refs_3_, bf16[4096,3584]{1,0:T(8,128)(2,1)} %all-gather.2.cloned.1.call-done.refs_0_.refs_1_.refs_2_.refs_3_, ...), custom_call_target="tpu_custom_call", output_to_operand_aliasing={{}: (9, {})} | custom-call | flops 7474999808 | tf_op jit(solution)/shard_map/product/pallas_call | solution.py:207
  525.0 15.9 %product.14.refs_8_ = f32[3584,3584]{1,0:T(8,128)} custom-call(s32[4]{0:T(128)S(1)} %and_select_fusion.at_ref, bf16[4096,3584]{1,0:T(8,128)(2,1)} %all-gather.2.cloned.1.call-done.refs_0_.refs_1_.refs_2_.refs_3_, bf16[4096,3584]{1,0:T(8,128)(2,1)} %all-gather.2.cloned.1.call-done.refs_0_.refs_1_.refs_2_.refs_3_, ...), custom_call_target="tpu_custom_call", output_to_operand_aliasing={{}: (9, {})} | custom-call | flops 5634999808 | tf_op jit(solution)/shard_map/product/pallas_call | solution.py:207
  541.0 15.7 %product.15 = f32[3584,3584]{1,0:T(8,128)} custom-call(s32[4]{0:T(128)S(1)} %and_select_fusion.at_ref, bf16[4096,3584]{1,0:T(8,128)(2,1)} %all-gather.2.cloned.1.call-done.refs_0_.refs_1_.refs_2_.refs_3_, bf16[4096,3584]{1,0:T(8,128)(2,1)} %all-gather.2.cloned.1.call-done.refs_0_.refs_1_.refs_2_.refs_3_, ...), custom_call_target="tpu_custom_call", output_to_operand_aliasing={{}: (9, {})} | custom-call | flops 5634999808 | tf_op jit(solution)/shard_map/product/pallas_call | solution.py:207
  (161 shorter events, 103.6 us)
Async XLA Ops:
  6.5 261.5 %all-gather.2.cloned.1.call-start = ((), (), s32[]{:S(2)}) async-start(), calls=%async_computation | async-start | bytes 36700160 | tf_op jit(solution)/shard_map/all_gather | solution.py:281
  51.8 56.8 %collective-permute-start.3 = (bf16[1024,512]{1,0:T(8,128)(2,1)}, bf16[1024,512]{1,0:T(8,128)(2,1)S(1)}, u32[]{:S(2)}, u32[]{:S(2)}) collective-permute-start(bf16[1024,512]{1,0:T(8,128)(2,1)} %bitcast.38), channel_id=1, source_target_pairs={{0,4},{4,8},{8,12},{12,0},{1,5},{5,9},{9,13},{13,1},{2,6},{6,10},{... | collective-permute-start | bytes 3145736 | tf_op jit(solution)/shard_map/ppermute | solution.py:273
  53.5 57.0 %collective-permute-start.4 = (bf16[1024,512]{1,0:T(8,128)(2,1)}, bf16[1024,512]{1,0:T(8,128)(2,1)}, u32[]{:S(2)}, u32[]{:S(2)}) collective-permute-start(bf16[1024,512]{1,0:T(8,128)(2,1)} %bitcast.39), channel_id=1, source_target_pairs={{0,12},{4,0},{8,4},{12,8},{1,13},{5,1},{9,5},{13,9},{2,14},{6,2},{... | collective-permute-start | bytes 3145736 | tf_op jit(solution)/shard_map/ppermute | solution.py:273
  104.8 50.7 %collective-permute-start.12 = (bf16[1024,512]{1,0:T(8,128)(2,1)}, bf16[1024,512]{1,0:T(8,128)(2,1)}, u32[]{:S(2)}, u32[]{:S(2)}) collective-permute-start(bf16[1024,512]{1,0:T(8,128)(2,1)} %bitcast.19), channel_id=1, source_target_pairs={{0,12},{4,0},{8,4},{12,8},{1,13},{5,1},{9,5},{13,9},{2,14},{6,2},{... | collective-permute-start | bytes 3145736 | tf_op jit(solution)/shard_map/ppermute | solution.py:273
  112.1 67.7 %collective-permute-start.16 = (bf16[1024,512]{1,0:T(8,128)(2,1)S(1)}, bf16[1024,512]{1,0:T(8,128)(2,1)S(1)}, u32[]{:S(2)}, u32[]{:S(2)}) collective-permute-start(bf16[1024,512]{1,0:T(8,128)(2,1)S(1)} %onward.8.refs_0_), channel_id=1, source_target_pairs={{0,4},{4,0},{8,12},{12,8},{1,5},{5,1},{9,13},{13,9},{2,6},{6,2},{1... | collective-permute-start | bytes 3145736 | tf_op jit(solution)/shard_map/ppermute | solution.py:278
  136.8 63.5 %collective-permute-start.22 = (bf16[1024,512]{1,0:T(8,128)(2,1)}, bf16[1024,512]{1,0:T(8,128)(2,1)S(1)}, u32[]{:S(2)}, u32[]{:S(2)}) collective-permute-start(bf16[1024,512]{1,0:T(8,128)(2,1)} %bitcast.22), channel_id=1, source_target_pairs={{0,4},{4,8},{8,12},{12,0},{1,5},{5,9},{9,13},{13,1},{2,6},{6,10},{... | collective-permute-start | bytes 3145736 | tf_op jit(solution)/shard_map/ppermute | solution.py:273
  137.7 83.3 %collective-permute-start.23 = (bf16[1024,512]{1,0:T(8,128)(2,1)}, bf16[1024,512]{1,0:T(8,128)(2,1)S(1)}, u32[]{:S(2)}, u32[]{:S(2)}) collective-permute-start(bf16[1024,512]{1,0:T(8,128)(2,1)} %bitcast.23), channel_id=1, source_target_pairs={{0,12},{4,0},{8,4},{12,8},{1,13},{5,1},{9,5},{13,9},{2,14},{6,2},{... | collective-permute-start | bytes 3145736 | tf_op jit(solution)/shard_map/ppermute | solution.py:273
  178.7 69.0 %collective-permute-start.24 = (bf16[1024,512]{1,0:T(8,128)(2,1)}, bf16[1024,512]{1,0:T(8,128)(2,1)S(1)}, u32[]{:S(2)}, u32[]{:S(2)}) collective-permute-start(bf16[1024,512]{1,0:T(8,128)(2,1)} %copy-done.15), channel_id=1, source_target_pairs={{0,4},{4,0},{8,12},{12,8},{1,5},{5,1},{9,13},{13,9},{2,6},{6,2},{1... | collective-permute-start | bytes 3145736 | tf_op jit(solution)/shard_map/ppermute | solution.py:278
  182.4 85.4 %collective-permute-start.17 = (bf16[1024,512]{1,0:T(8,128)(2,1)}, bf16[1024,512]{1,0:T(8,128)(2,1)S(1)}, u32[]{:S(2)}, u32[]{:S(2)}) collective-permute-start(bf16[1024,512]{1,0:T(8,128)(2,1)} %bitcast.26), channel_id=1, source_target_pairs={{0,4},{4,8},{8,12},{12,0},{1,5},{5,9},{9,13},{13,1},{2,6},{6,10},{... | collective-permute-start | bytes 3145736 | tf_op jit(solution)/shard_map/ppermute | solution.py:273
  200.3 46.9 %collective-permute-start.20 = (bf16[256,512]{1,0:T(8,128)(2,1)S(1)}, bf16[256,512]{1,0:T(8,128)(2,1)S(1)}, u32[]{:S(2)}, u32[]{:S(2)}) collective-permute-start(bf16[256,512]{1,0:T(8,128)(2,1)S(1)} %get-tuple-element.51), channel_id=1, source_target_pairs={{0,2},{1,3},{2,0},{3,1},{4,6},{5,7},{6,4},{7,5},{8,10},{9,11},{10,... | collective-permute-start | bytes 786440 | tf_op jit(solution)/shard_map/ppermute | solution.py:230
  224.7 65.8 %collective-permute-start.18 = (bf16[1024,512]{1,0:T(8,128)(2,1)}, bf16[1024,512]{1,0:T(8,128)(2,1)}, u32[]{:S(2)}, u32[]{:S(2)}) collective-permute-start(bf16[1024,512]{1,0:T(8,128)(2,1)} %bitcast.28), channel_id=1, source_target_pairs={{0,12},{4,0},{8,4},{12,8},{1,13},{5,1},{9,5},{13,9},{2,14},{6,2},{... | collective-permute-start | bytes 3145736 | tf_op jit(solution)/shard_map/ppermute | solution.py:273
  247.3 69.9 %collective-permute-start.33 = (bf16[1024,512]{1,0:T(8,128)(2,1)}, bf16[1024,512]{1,0:T(8,128)(2,1)}, u32[]{:S(2)}, u32[]{:S(2)}) collective-permute-start(bf16[1024,512]{1,0:T(8,128)(2,1)} %copy-done.13), channel_id=1, source_target_pairs={{0,4},{4,0},{8,12},{12,8},{1,5},{5,1},{9,13},{13,9},{2,6},{6,2},{1... | collective-permute-start | bytes 3145736 | tf_op jit(solution)/shard_map/ppermute | solution.py:278
  247.4 47.4 %collective-permute-start.30 = (bf16[256,512]{1,0:T(8,128)(2,1)S(1)}, bf16[256,512]{1,0:T(8,128)(2,1)S(1)}, u32[]{:S(2)}, u32[]{:S(2)}) collective-permute-start(bf16[256,512]{1,0:T(8,128)(2,1)S(1)} %get-tuple-element.58), channel_id=1, source_target_pairs={{0,1},{1,0},{2,3},{3,2},{4,5},{5,4},{6,7},{7,6},{8,9},{9,8},{10,11... | collective-permute-start | bytes 786440 | tf_op jit(solution)/shard_map/ppermute | solution.py:230
  250.2 85.2 %collective-permute-start.28 = (bf16[1024,512]{1,0:T(8,128)(2,1)}, bf16[1024,512]{1,0:T(8,128)(2,1)}, u32[]{:S(2)}, u32[]{:S(2)}) collective-permute-start(bf16[1024,512]{1,0:T(8,128)(2,1)} %bitcast.10), channel_id=1, source_target_pairs={{0,4},{4,8},{8,12},{12,0},{1,5},{5,9},{9,13},{13,1},{2,6},{6,10},{... | collective-permute-start | bytes 3145736 | tf_op jit(solution)/shard_map/ppermute | solution.py:273
  267.8 88.1 %collective-permute-start.29 = (bf16[1024,512]{1,0:T(8,128)(2,1)}, bf16[1024,512]{1,0:T(8,128)(2,1)}, u32[]{:S(2)}, u32[]{:S(2)}) collective-permute-start(bf16[1024,512]{1,0:T(8,128)(2,1)} %bitcast.11), channel_id=1, source_target_pairs={{0,12},{4,0},{8,4},{12,8},{1,13},{5,1},{9,5},{13,9},{2,14},{6,2},{... | collective-permute-start | bytes 3145736 | tf_op jit(solution)/shard_map/ppermute | solution.py:273
  315.1 90.4 %collective-permute-start.35 = (bf16[1024,512]{1,0:T(8,128)(2,1)}, bf16[1024,512]{1,0:T(8,128)(2,1)S(1)}, u32[]{:S(2)}, u32[]{:S(2)}) collective-permute-start(bf16[1024,512]{1,0:T(8,128)(2,1)} %copy-done.14), channel_id=1, source_target_pairs={{0,4},{4,0},{8,12},{12,8},{1,5},{5,1},{9,13},{13,9},{2,6},{6,2},{1... | collective-permute-start | bytes 3145736 | tf_op jit(solution)/shard_map/ppermute | solution.py:278
  318.8 92.3 %collective-permute-start.36 = (bf16[1024,512]{1,0:T(8,128)(2,1)}, bf16[1024,512]{1,0:T(8,128)(2,1)}, u32[]{:S(2)}, u32[]{:S(2)}) collective-permute-start(bf16[1024,512]{1,0:T(8,128)(2,1)} %bitcast.14), channel_id=1, source_target_pairs={{0,4},{4,8},{8,12},{12,0},{1,5},{5,9},{9,13},{13,1},{2,6},{6,10},{... | collective-permute-start | bytes 3145736 | tf_op jit(solution)/shard_map/ppermute | solution.py:273
  318.8 104.5 %collective-permute-start.37 = (bf16[1024,512]{1,0:T(8,128)(2,1)}, bf16[1024,512]{1,0:T(8,128)(2,1)}, u32[]{:S(2)}, u32[]{:S(2)}) collective-permute-start(bf16[1024,512]{1,0:T(8,128)(2,1)} %bitcast.15), channel_id=1, source_target_pairs={{0,12},{4,0},{8,4},{12,8},{1,13},{5,1},{9,5},{13,9},{2,14},{6,2},{... | collective-permute-start | bytes 3145736 | tf_op jit(solution)/shard_map/ppermute | solution.py:273
  335.4 46.5 %collective-permute-start.25 = (bf16[256,512]{1,0:T(8,128)(2,1)S(1)}, bf16[256,512]{1,0:T(8,128)(2,1)S(1)}, u32[]{:S(2)}, u32[]{:S(2)}) collective-permute-start(bf16[256,512]{1,0:T(8,128)(2,1)S(1)} %get-tuple-element.55), channel_id=1, source_target_pairs={{0,1},{1,0},{2,3},{3,2},{4,5},{5,4},{6,7},{7,6},{8,9},{9,8},{10,11... | collective-permute-start | bytes 786440 | tf_op jit(solution)/shard_map/ppermute | solution.py:230
  382.0 66.5 %collective-permute-start.34 = (bf16[1024,512]{1,0:T(8,128)(2,1)S(1)}, bf16[1024,512]{1,0:T(8,128)(2,1)S(1)}, u32[]{:S(2)}, u32[]{:S(2)}) collective-permute-start(bf16[1024,512]{1,0:T(8,128)(2,1)S(1)} %onward.12.refs_9_), channel_id=1, source_target_pairs={{0,4},{4,0},{8,12},{12,8},{1,5},{5,1},{9,13},{13,9},{2,6},{6,2},{1... | collective-permute-start | bytes 3145736 | tf_op jit(solution)/shard_map/ppermute | solution.py:278
  407.2 51.7 %collective-permute-start.38 = (bf16[1024,256]{1,0:T(8,128)(2,1)S(1)}, bf16[1024,256]{1,0:T(8,128)(2,1)S(1)}, u32[]{:S(2)}, u32[]{:S(2)}) collective-permute-start(bf16[1024,256]{1,0:T(8,128)(2,1)S(1)} %bitcast.34), channel_id=1, source_target_pairs={{0,4},{4,8},{8,12},{12,0},{1,5},{5,9},{9,13},{13,1},{2,6},{6,10},{... | collective-permute-start | bytes 1572872 | tf_op jit(solution)/shard_map/ppermute | solution.py:273
  408.4 59.8 %collective-permute-start.39 = (bf16[1024,256]{1,0:T(8,128)(2,1)S(1)}, bf16[1024,256]{1,0:T(8,128)(2,1)S(1)}, u32[]{:S(2)}, u32[]{:S(2)}) collective-permute-start(bf16[1024,256]{1,0:T(8,128)(2,1)S(1)} %bitcast.35), channel_id=1, source_target_pairs={{0,12},{4,0},{8,4},{12,8},{1,13},{5,1},{9,5},{13,9},{2,14},{6,2},{... | collective-permute-start | bytes 1572872 | tf_op jit(solution)/shard_map/ppermute | solution.py:273
  424.9 66.6 %collective-permute-start.40 = (bf16[1024,512]{1,0:T(8,128)(2,1)S(1)}, bf16[1024,512]{1,0:T(8,128)(2,1)S(1)}, u32[]{:S(2)}, u32[]{:S(2)}) collective-permute-start(bf16[1024,512]{1,0:T(8,128)(2,1)S(1)} %onward.13.refs_9_), channel_id=1, source_target_pairs={{0,4},{4,0},{8,12},{12,8},{1,5},{5,1},{9,13},{13,9},{2,6},{6,2},{1... | collective-permute-start | bytes 3145736 | tf_op jit(solution)/shard_map/ppermute | solution.py:278
  469.0 55.2 %collective-permute-start.44 = (bf16[1024,256]{1,0:T(8,128)(2,1)}, bf16[1024,256]{1,0:T(8,128)(2,1)}, u32[]{:S(2)}, u32[]{:S(2)}) collective-permute-start(bf16[1024,256]{1,0:T(8,128)(2,1)} %onward.14.refs_9_), channel_id=1, source_target_pairs={{0,4},{4,0},{8,12},{12,8},{1,5},{5,1},{9,13},{13,9},{2,6},{6,2},{1... | collective-permute-start | bytes 1572872 | tf_op jit(solution)/shard_map/ppermute | solution.py:278
  (51 other events, 1022.0 us)
Sparse Core Ops, SparseCore 0:
  35.0 225.6 all-gather.1
